TPU v7x, 32 devices: a whole 2x2x4 slice. The times are simulated.
32 devices in a mesh: dom: 16 (over z, y, x), rep: 2 (over core).
Axes of the slice: x: 2, y: 2, z: 4, core: 2. Of those that a mesh axis runs over, the one named last changes fastest.
Arguments:
- features: bfloat16 [4096, 256], P(('dom', 'rep')), may hold values from -6 to 6
- block_values: bfloat16 [32, 16, 2, 128, 128], P(('dom', 'rep'))
- block_columns: int32 [32, 16, 2], P(('dom', 'rep')), may hold values from 0 to 15, as said below
- weight: bfloat16 [256, 256], replicated, may hold values from -0.375 to 0.375
- cotangent: bfloat16 [4096, 256], P(('dom', 'rep')), may hold values from -6 to 6
Outputs:
- feature_grad: bfloat16 [4096, 256], P(('dom', 'rep'))
- weight_grad: float32 [256, 256], replicated
Inputs may be any that keep to these rules, and one draw needn't show every extreme that they name: Slot (t, a) of the device with dom index d and rep index r lies at block row d * 2 + a and block column block_columns * 2 + r. The adjacency is symmetric: each slot at block row p and block column q has a partner slot of the same t at block row q and block column p whose block_values are its transpose; a slot with p equal to q holds a symmetric block.
All inputs are finite; a program needn't handle non-finite values.
Results may differ from a plain program's by a relative error of at most 0.006.
Values may be sent and summed in bfloat16 or wider, within the bound.
A program may use at most 64 MiB of HBM per device.

v0:
```python
import math

import jax
import jax.numpy as jnp
from jax import lax
from jax.sharding import PartitionSpec as P


def panel_product(values, columns, gathered, block_rows):
    panel_count = gathered.shape[0] // block_rows
    panels = gathered.reshape(panel_count, block_rows, gathered.shape[1])
    picked = panels[columns]
    summed = jnp.einsum("taij,tajf->aif", values, picked, preferred_element_type=jnp.float32)
    return summed.reshape(-1, summed.shape[-1])


def dense_grads(hidden, weight, cotangent):
    pre_act = jnp.dot(hidden, weight, preferred_element_type=jnp.float32)
    sigmoid_value = jax.nn.sigmoid(pre_act)
    slope_value = sigmoid_value * (1.0 + pre_act * (1.0 - sigmoid_value))
    grad_pre = (cotangent.astype(jnp.float32) * slope_value).astype(jnp.bfloat16)
    hidden_grad = jnp.einsum(
        "rg,fg->rf", grad_pre, weight, preferred_element_type=jnp.float32
    ).astype(jnp.bfloat16)
    weight_part = jnp.einsum("rf,rg->fg", hidden, grad_pre, preferred_element_type=jnp.float32)
    return (hidden_grad, weight_part)


def shards(features, block_values, block_columns, weight, cotangent):
    block_rows = features.shape[0]
    values = block_values[0]
    columns = block_columns[0]
    rep_index = lax.axis_index("rep")
    gathered = lax.all_gather(features, "dom", axis=0, tiled=True)
    node_total = gathered.shape[0] * lax.axis_size("rep")
    inv_scale = 1.0 / math.sqrt(node_total)
    partial_value = panel_product(values, columns, gathered, block_rows)
    hidden = lax.psum(partial_value, "rep").astype(jnp.bfloat16)
    whole_cotangent = lax.all_gather(cotangent, "rep", axis=0, tiled=True)
    hidden_grad, weight_part = dense_grads(hidden, weight, whole_cotangent)
    weight_grad = lax.psum(weight_part, "dom") * inv_scale
    own_grad = lax.dynamic_slice_in_dim(hidden_grad, rep_index * block_rows, block_rows, 0)
    grad_rows = lax.all_gather(own_grad, "dom", axis=0, tiled=True)
    back_partial = panel_product(values, columns, grad_rows, block_rows)
    grad_sum = lax.psum(back_partial, "rep")
    feature_grad = lax.dynamic_slice_in_dim(grad_sum, rep_index * block_rows, block_rows, 0)
    return (feature_grad.astype(jnp.bfloat16), weight_grad)


def solution(mesh):
    return jax.shard_map(
        shards,
        mesh=mesh,
        in_specs=(
            P(("dom", "rep"), None),
            P(("dom", "rep"), None, None, None, None),
            P(("dom", "rep"), None, None),
            P(),
            P(("dom", "rep"), None),
        ),
        out_specs=(P(("dom", "rep"), None), P()),
        check_vma=False,
    )
```

profile of v0, /device:TPU:1, one launch (start us, length us, event | category | flops | bytes accessed | tf_op | source)
XLA Modules:
  0.0 254.9 jit_solution(13762039094952908429)
XLA Ops:
  7.2 0.0 all-gather.3.cloned.1.call-start
  7.2 0.7 all-gather.3.cloned.1.call-update
  7.9 0.0 all-reduce.4.cloned.1.call-start
  8.0 0.7 compare_select_fusion
  8.6 0.1 copy.10
  8.7 0.1 reshape.50
  8.8 3.4 %all_gather.9 = bf16[256,256]{1,0:T(8,128)(2,1)} all-gather(bf16[128,256]{1,0:T(8,128)(2,1)} %param.9), channel_id=1, replica_groups=mesh['dom'=16,'rep'=2] {'rep'}, dimensions={0}, use_global_device_ids=true | all-gather | bytes 196608 | tf_op jit(solution)/shard_map/all_gather | solution.py:39
  12.2 54.7 %all-gather.3.cloned.1.call-done = bf16[2048,256]{1,0:T(8,128)(2,1)} async-done(((bf16[128,256]{1,0:T(8,128)(2,1)}), bf16[2048,256]{1,0:T(8,128)(2,1)}) %all-gather.3.cloned.1.call-update) | async-done | bytes 1048592 | tf_op jit(solution)/shard_map/all_gather | solution.py:34
  66.9 1.9 gather_fusion
  68.8 0.4 fusion
  69.2 6.0 %all-reduce.5 = bf16[256,256]{1,0:T(8,128)(2,1)S(1)} all-reduce(f32[256,256]{1,0:T(8,128)S(1)} %bitcast.35), channel_id=1, replica_groups=mesh['dom'=16,'rep'=2] {'rep'}, use_global_device_ids=true, to_apply=%region_0.0 | all-reduce | flops 65536 | bytes 393216 | tf_op jit(solution)/shard_map/psum | solution.py:38
  75.3 1.2 multiply_convert_fusion
  76.4 0.9 fusion.11
  77.3 0.0 all-reduce.4.cloned.1.call-update
  77.4 0.0 all-gather.5.cloned.1.call-start
  77.4 0.2 fusion.10
  77.7 0.6 dynamic-slice_convert_fusion
  78.3 102.5 %all-reduce.4.cloned.1.call-done = f32[256,256]{1,0:T(8,128)} async-done(((f32[256,256]{1,0:T(8,128)}), f32[256,256]{1,0:T(8,128)}) %all-reduce.4.cloned.1.call-update) | async-done | bytes 262160 | tf_op jit(solution)/shard_map/psum | solution.py:41
  180.8 1.7 broadcast_multiply_fusion
  182.4 56.9 %all-gather.5.cloned.1.call-done = bf16[2048,256]{1,0:T(8,128)(2,1)} async-done(((bf16[128,256]{1,0:T(8,128)(2,1)}), bf16[2048,256]{1,0:T(8,128)(2,1)}) %all-gather.5.cloned.1.call-update) | async-done | bytes 1048592 | tf_op jit(solution)/shard_map/all_gather | solution.py:43
  239.3 1.9 gather_fusion.1
  241.3 0.4 fusion.2
  241.7 6.0 %all-reduce.6 = bf16[256,256]{1,0:T(8,128)(2,1)S(1)} all-reduce(f32[256,256]{1,0:T(8,128)S(1)} %bitcast.36), channel_id=1, replica_groups=mesh['dom'=16,'rep'=2] {'rep'}, use_global_device_ids=true, to_apply=%region_1.0 | all-reduce | flops 65536 | bytes 393216 | tf_op jit(solution)/shard_map/psum | solution.py:45
  247.7 0.6 dynamic-slice_convert_fusion.1
  (6 shorter events, 0.0 us)
Async XLA Ops:
  7.2 61.6 %copy-start = (bf16[1,16,2,128,128]{4,3,2,1,0:T(8,128)(2,1)S(1)}, bf16[1,16,2,128,128]{4,3,2,1,0:T(8,128)(2,1)}, u32[]{:S(2)}) copy-start(bf16[1,16,2,128,128]{4,3,2,1,0:T(8,128)(2,1)} %param.6) | copy-start | bytes 3145732
  7.2 59.7 %all-gather.3.cloned.1.call-start = ((), (), s32[]{:S(2)}) async-start(), calls=%async_computation | async-start | bytes 1114112 | tf_op jit(solution)/shard_map/all_gather | solution.py:34
  7.9 172.9 %all-reduce.4.cloned.1.call-start = ((), (), s32[]{:S(2)}) async-start(), calls=%async_computation.2 | async-start | bytes 524288 | tf_op jit(solution)/shard_map/psum | solution.py:41
  68.8 6.5 %copy-start.1 = (bf16[256,256]{1,0:T(8,128)(2,1)S(1)}, bf16[256,256]{1,0:T(8,128)(2,1)}, u32[]{:S(2)}) copy-start(bf16[256,256]{1,0:T(8,128)(2,1)} %param.8) | copy-start | bytes 393220
  77.4 162.0 %all-gather.5.cloned.1.call-start = ((), (), s32[]{:S(2)}) async-start(), calls=%async_computation.1 | async-start | bytes 1114112 | tf_op jit(solution)/shard_map/all_gather | solution.py:43
Sparse Core Ops, SparseCore 0:
  10.8 56.0 all-gather.2
  77.5 103.2 all-reduce.3
  184.5 54.8 all-gather.4
where the time goes:
time: 255 us
  waiting for transfers between devices  215 us (84%)
  blocking collectives  15.3 us (6%)
  between operations  13.8 us (5%)
  local copies, waits for them, and re-layouts  5.28 us (2%)
  matrix products  3.19 us (1%)
    psum x1, waiting for transfers between devices, shards(): weight_grad = lax.psum(weight_part, 'dom') * inv_scale  102 us
    all_gather x1, waiting for transfers between devices, shards(): grad_rows = lax.all_gather(own_grad, 'dom', axis=0, tiled=True)  56.9 us
    all_gather x1, waiting for transfers between devices, shards(): gathered = lax.all_gather(features, 'dom', axis=0, tiled=True)  54.7 us
    psum x1, blocking collectives, shards(): hidden = lax.psum(partial_value, 'rep').astype(jnp.bfloat16)  5.99 us
    psum x1, blocking collectives, shards(): grad_sum = lax.psum(back_partial, 'rep')  5.99 us
  transfers between devices with their start and end apart: 3, of which 3 were waited for; matrix products, arithmetic and copies ran while one was open for 1% of the time, Pallas kernels for 0%

commit v1 on v0

v1 whole, which is shorter than its diff:
```python
import functools
import math

import jax
import jax.numpy as jnp
from jax import lax
from jax.experimental import pallas as pl
from jax.experimental.pallas import tpu as pltpu
from jax.sharding import PartitionSpec as P

MESH = pl.DeviceIdType.MESH
FACE = 4
SUBLANES = 8


def flip(index, offset):
    result, bit = index, 1
    while bit <= offset:
        if offset & bit:
            result = result + bit - 2 * bit * ((index // bit) % 2)
        bit *= 2
    return result


def silu_slope(pre_act):
    sigmoid_value = jax.nn.sigmoid(pre_act)
    return sigmoid_value * (1.0 + pre_act * (1.0 - sigmoid_value))


class Sends:
    def __init__(self):
        self.started = []

    def start(self, src, dst, send_sem, recv_sem, target):
        copy = pltpu.make_async_remote_copy(
            src_ref=src, dst_ref=dst, send_sem=send_sem, recv_sem=recv_sem,
            device_id=target, device_id_type=MESH,
        )
        copy.start()
        self.started.append(copy)

    def finish(self):
        for copy in self.started:
            copy.wait_send()


def arrived(ref, send_sem, recv_sem, target):
    pltpu.make_async_remote_copy(
        src_ref=ref, dst_ref=ref, send_sem=send_sem, recv_sem=recv_sem,
        device_id=target, device_id_type=MESH,
    ).wait_recv()


def kernel(
    n_dom, n_rep, inv_scale,
    columns_ref, features_ref, values_hbm, weight_ref, cotangent_ref,
    feature_grad_ref, weight_grad_ref,
    values_ref, panels, grad_panels, own_grad, part_out, part_in,
    weight_part, weight_in1, weight_sum1, weight_in2, weight_sum2, weight_in3, weight_out,
    values_sem, gather_send, gather_recv, part_send, part_recv, weight_send, weight_recv,
):
    rows = features_ref.shape[0]
    half = rows // 2
    rounds = values_ref.shape[0]
    line = n_dom // FACE
    dom, rep = lax.axis_index("dom"), lax.axis_index("rep")
    z, face = dom // FACE, dom % FACE

    def panel_at(z_at, face_at):
        return z_at * FACE + face_at

    line_ids = [panel_at(flip(z, k), face) for k in range(line)]
    face_ids = [panel_at(z, flip(face, j)) for j in range(FACE)]
    rep_ids = [lax.rem(rep + k, n_rep) for k in range(n_rep)]
    from_rep_ids = [lax.rem(rep - k + n_rep, n_rep) for k in range(n_rep)]
    line_to = [{"dom": i} for i in line_ids]
    face_to = [{"dom": i} for i in face_ids]
    rep_to = [{"rep": i} for i in rep_ids]

    values_copy = pltpu.make_async_copy(values_hbm.at[0], values_ref, values_sem)
    values_copy.start()

    barrier = pltpu.get_barrier_semaphore()
    partners = line_to[1:] + face_to[1:] + rep_to[1:]
    for target in partners:
        pl.semaphore_signal(barrier, inc=1, device_id=target, device_id_type=MESH)
    pl.semaphore_wait(barrier, len(partners))

    sends = Sends()

    def gather(which, own_ref, held):
        send_sem, recv_sem = gather_send.at[which], gather_recv.at[which]
        line_at, full_at, half_at = 0, (line, 2 * line), (3 * line, 4 * line)
        halves = (pl.ds(0, half), pl.ds(half, half))

        def sem_pair(at):
            return send_sem.at[at], recv_sem.at[at]

        def to_neighbours(k):
            panel = line_ids[k]
            src = own_ref if k == 0 else held.at[panel]
            for way in range(2):
                sends.start(src, held.at[panel], *sem_pair(full_at[way] + k), face_to[way + 1])

        def to_diagonal(k):
            for way in range(2):
                panel = panel_at(flip(z, k), flip(face, way + 1))
                arrived(held.at[panel], *sem_pair(full_at[way] + k), face_to[way + 1])
                piece = held.at[panel, halves[way]]
                sends.start(piece, piece, *sem_pair(half_at[1 - way] + k), face_to[2 - way])

        def begin():
            for k in range(1, line):
                sends.start(own_ref, held.at[dom], *sem_pair(line_at + k), line_to[k])
            to_neighbours(0)
            held[dom] = own_ref[...]

        def middle(k):
            arrived(held.at[line_ids[k]], *sem_pair(line_at + k), line_to[k])
            to_neighbours(k)
            to_diagonal(k - 1)

        def finish():
            for k in range(line):
                panel = panel_at(flip(z, k), flip(face, 3))
                for way in range(2):
                    arrived(held.at[panel, halves[1 - way]], *sem_pair(half_at[way] + k), face_to[way + 1])

        steps = [begin]
        steps += [functools.partial(middle, k) for k in range(1, line)]
        steps += [functools.partial(to_diagonal, line - 1), finish]
        return steps

    def block_product(held, a):
        left = jnp.concatenate([values_ref[t, a] for t in range(rounds)], axis=1)
        right = jnp.concatenate([held[columns_ref[0, t, a]] for t in range(rounds)], axis=0)
        return jnp.dot(left, right, preferred_element_type=jnp.float32)

    def panel_start(which, held):
        for k in range(1, n_rep):
            part_out[which, k - 1] = block_product(held, rep_ids[k])
            sends.start(
                part_out.at[which, k - 1], part_in.at[which, k - 1],
                part_send.at[which, k - 1], part_recv.at[which, k - 1], rep_to[k],
            )
        return block_product(held, rep)

    def panel_end(which, total):
        for k in range(1, n_rep):
            arrived(
                part_in.at[which, k - 1], part_send.at[which, k - 1],
                part_recv.at[which, k - 1], rep_to[k],
            )
            total = total + part_in[which, k - 1]
        return total.astype(jnp.bfloat16)

    for step in gather(0, features_ref, panels):
        step()
    values_copy.wait()
    hidden = panel_end(0, panel_start(0, panels))

    weight = weight_ref[...]
    pre_act = jnp.dot(hidden, weight, preferred_element_type=jnp.float32)
    grad_pre = (cotangent_ref[...].astype(jnp.float32) * silu_slope(pre_act)).astype(jnp.bfloat16)
    own_grad[...] = lax.dot_general(
        grad_pre, weight, (((1,), (1,)), ((), ())), preferred_element_type=jnp.float32
    ).astype(jnp.bfloat16)
    back = gather(1, own_grad, grad_panels)
    back[0]()

    rep_rows = weight.shape[0] // n_rep
    line_rows = rep_rows // line
    face_rows = line_rows // FACE
    rep_base = rep * rep_rows
    line_base = rep_base + z * line_rows
    sem_at = [0]

    def weight_sems(count):
        base = sem_at[0]
        sem_at[0] += count - 1
        return [(weight_send.at[base + k - 1], weight_recv.at[base + k - 1]) for k in range(1, count)]

    def span(start, size):
        return pl.ds(pl.multiple_of(start, SUBLANES), size)

    def exchange(out_ref, in_ref, targets, ids, size):
        sems = weight_sems(len(targets))
        for k in range(1, len(targets)):
            sends.start(out_ref.at[span(ids[k] * size, size)], in_ref.at[k - 1], *sems[k - 1], targets[k])
        return sems

    def take(in_ref, sems, targets, total):
        for k in range(1, len(targets)):
            arrived(in_ref.at[k - 1], *sems[k - 1], targets[k])
            total = total + in_ref[k - 1]
        return total

    def share(start, size, targets):
        sems = weight_sems(len(targets))
        piece = weight_out.at[span(start, size)]
        for k in range(1, len(targets)):
            sends.start(piece, piece, *sems[k - 1], targets[k])
        return sems

    def collect(starts, size, sems, targets):
        for k in range(1, len(targets)):
            arrived(weight_out.at[span(starts[k], size)], *sems[k - 1], targets[k])

    line_z = [flip(z, k) for k in range(line)]
    face_f = [flip(face, j) for j in range(FACE)]

    weight_part[...] = lax.dot_general(
        hidden, grad_pre, (((0,), (0,)), ((), ())), preferred_element_type=jnp.float32
    )
    sems1 = exchange(weight_part, weight_in1, rep_to, rep_ids, rep_rows)
    back[1]()
    weight_sum1[...] = take(weight_in1, sems1, rep_to, weight_part[span(rep_base, rep_rows)])
    sems2 = exchange(weight_sum1, weight_in2, line_to, line_z, line_rows)
    for step in back[2:line]:
        step()
    weight_sum2[...] = take(weight_in2, sems2, line_to, weight_sum1[span(z * line_rows, line_rows)])
    sems3 = exchange(weight_sum2, weight_in3, face_to, face_f, face_rows)
    back[line]()
    own_sum = take(weight_in3, sems3, face_to, weight_sum2[span(face * face_rows, face_rows)])
    own_base = line_base + face * face_rows
    weight_out[span(own_base, face_rows)] = own_sum * inv_scale
    sems4 = share(own_base, face_rows, face_to)
    back[line + 1]()
    collect([line_base + f * face_rows for f in face_f], face_rows, sems4, face_to)
    sems5 = share(line_base, line_rows, line_to)

    total = panel_start(1, grad_panels)
    collect([rep_base + i * line_rows for i in line_z], line_rows, sems5, line_to)
    sems6 = share(rep_base, rep_rows, rep_to)
    feature_grad_ref[...] = panel_end(1, total)
    collect([i * rep_rows for i in from_rep_ids], rep_rows, sems6, rep_to)
    weight_grad_ref[...] = weight_out[...]
    sends.finish()


def kernel_shards(features, block_values, block_columns, weight, cotangent):
    n_dom, n_rep = lax.axis_size("dom"), lax.axis_size("rep")
    rows, width = features.shape
    _, rounds, _, blk, _ = block_values.shape
    wide = weight.shape[0]
    line = n_dom // FACE
    rep_rows = wide // n_rep
    line_rows = rep_rows // line
    face_rows = line_rows // FACE
    inv_scale = 1.0 / math.sqrt(rows * n_dom * n_rep)
    gather_copies = 5 * line
    weight_copies = 2 * ((n_rep - 1) + (line - 1) + (FACE - 1))
    vmem = pl.BlockSpec(memory_space=pltpu.VMEM)
    dma = pltpu.SemaphoreType.DMA
    parts = max(n_rep - 1, 1)
    return pl.pallas_call(
        functools.partial(kernel, n_dom, n_rep, inv_scale),
        out_shape=(
            jax.ShapeDtypeStruct((rows, width), jnp.bfloat16),
            jax.ShapeDtypeStruct(weight.shape, jnp.float32),
        ),
        in_specs=[
            pl.BlockSpec(memory_space=pltpu.SMEM), vmem, pl.BlockSpec(memory_space=pl.ANY), vmem, vmem,
        ],
        out_specs=(vmem, vmem),
        scratch_shapes=[
            pltpu.VMEM(block_values.shape[1:], jnp.bfloat16),
            pltpu.VMEM((n_dom, rows, width), jnp.bfloat16),
            pltpu.VMEM((n_dom, rows, width), jnp.bfloat16),
            pltpu.VMEM((rows, width), jnp.bfloat16),
            pltpu.VMEM((2, parts, rows, width), jnp.float32),
            pltpu.VMEM((2, parts, rows, width), jnp.float32),
            pltpu.VMEM(weight.shape, jnp.float32),
            pltpu.VMEM((parts, rep_rows, wide), jnp.float32),
            pltpu.VMEM((rep_rows, wide), jnp.float32),
            pltpu.VMEM((max(line - 1, 1), line_rows, wide), jnp.float32),
            pltpu.VMEM((line_rows, wide), jnp.float32),
            pltpu.VMEM((FACE - 1, face_rows, wide), jnp.float32),
            pltpu.VMEM(weight.shape, jnp.float32),
            dma,
            dma((2, gather_copies)),
            dma((2, gather_copies)),
            dma((2, parts)),
            dma((2, parts)),
            dma((weight_copies,)),
            dma((weight_copies,)),
        ],
        compiler_params=pltpu.CompilerParams(
            collective_id=0, has_side_effects=True, vmem_limit_bytes=32 * 1024 * 1024
        ),
    )(block_columns, features, block_values, weight, cotangent)


def panel_product(values, columns, gathered, block_rows):
    panel_count = gathered.shape[0] // block_rows
    panels = gathered.reshape(panel_count, block_rows, gathered.shape[1])
    picked = panels[columns]
    summed = jnp.einsum("taij,tajf->aif", values, picked, preferred_element_type=jnp.float32)
    return summed.reshape(-1, summed.shape[-1])


def plain_shards(features, block_values, block_columns, weight, cotangent):
    block_rows = features.shape[0]
    values, columns = block_values[0], block_columns[0]
    gathered = lax.all_gather(features, "dom", axis=0, tiled=True)
    inv_scale = 1.0 / math.sqrt(gathered.shape[0] * lax.axis_size("rep"))
    partial_value = panel_product(values, columns, gathered, block_rows)
    hidden = lax.psum_scatter(partial_value, "rep", scatter_dimension=0, tiled=True).astype(jnp.bfloat16)
    pre_act = jnp.dot(hidden, weight, preferred_element_type=jnp.float32)
    grad_pre = (cotangent.astype(jnp.float32) * silu_slope(pre_act)).astype(jnp.bfloat16)
    hidden_grad = jnp.einsum(
        "rg,fg->rf", grad_pre, weight, preferred_element_type=jnp.float32
    ).astype(jnp.bfloat16)
    weight_part = jnp.einsum("rf,rg->fg", hidden, grad_pre, preferred_element_type=jnp.float32)
    weight_grad = lax.psum(weight_part, ("dom", "rep")) * inv_scale
    grad_rows = lax.all_gather(hidden_grad, "dom", axis=0, tiled=True)
    back_partial = panel_product(values, columns, grad_rows, block_rows)
    feature_grad = lax.psum_scatter(back_partial, "rep", scatter_dimension=0, tiled=True)
    return (feature_grad.astype(jnp.bfloat16), weight_grad)


def shards(features, block_values, block_columns, weight, cotangent):
    n_dom, n_rep = lax.axis_size("dom"), lax.axis_size("rep")
    line = n_dom // FACE
    splits = (
        n_dom % FACE == 0
        and line & (line - 1) == 0
        and weight.shape[0] % (SUBLANES * n_dom * n_rep) == 0
    )
    body = kernel_shards if splits else plain_shards
    return body(features, block_values, block_columns, weight, cotangent)


def solution(mesh):
    return jax.shard_map(
        shards,
        mesh=mesh,
        in_specs=(
            P(("dom", "rep"), None),
            P(("dom", "rep"), None, None, None, None),
            P(("dom", "rep"), None, None),
            P(),
            P(("dom", "rep"), None),
        ),
        out_specs=(P(("dom", "rep"), None), P()),
        check_vma=False,
    )
```

time: 255 us -> 52.5 us (0.21)
  waiting for transfers between devices: 215 us -> 0 us
  Pallas kernels: 0 us -> 45.7 us
  blocking collectives: 15.3 us -> 0 us
  between operations: 13.8 us -> 0.64 us
  matrix products: 3.19 us -> 0 us
    all_gather x2 -> x0, waiting for transfers between devices: 112 us -> none  [the longest x1 56.9 us: shards(): grad_rows = lax.all_gather(own_grad, 'dom', axis=0, tiled=True)]
    psum x1 -> x0, waiting for transfers between devices: 102 us -> none  [shards(): weight_grad = lax.psum(weight_part, 'dom') * inv_scale]
    pallas_call x0 -> x1, Pallas kernels: none -> 45.7 us  [kernel_shards(): pl.pallas_call(functools.partial(kernel, n_dom, n_rep, inv_scale), out_sh...]
    psum x2 -> x0, blocking collectives: 12 us -> none  [the longest x1 5.99 us: shards(): hidden = lax.psum(partial_value, 'rep').astype(jnp.bfloat16)]
    unnamed x4 -> x11, local copies, waits for them, and re-layouts: 0.02 us -> 5.9 us
    gather x2 -> x0, local copies, waits for them, and re-layouts: 3.81 us -> none  [panel_product(): picked = panels[columns]]
    all_gather x1 -> x0, blocking collectives: 3.36 us -> none  [shards(): whole_cotangent = lax.all_gather(cotangent, 'rep', axis=0, tiled=True)]
    dot_general x5 -> x0, matrix products: 3.19 us -> none  [the longest x1 1.16 us: dense_grads(): pre_act = jnp.dot(hidden, weight, preferred_element_type=jnp.float32)]
  transfers between devices with their start and end apart: 3 -> 0, of which waited for: 3 -> 0; matrix products, arithmetic and copies ran while one was open for 1% -> 0% of each run, Pallas kernels for 0% -> 0%
where the time goes in v1:
time: 52.5 us; the launch traced here: 52.2 us
  Pallas kernels  45.7 us (87%)
  local copies, waits for them, and re-layouts  5.9 us (11%)
  between operations  0.64 us (1%)
    pallas_call x1, Pallas kernels, kernel_shards(): pl.pallas_call(functools.partial(kernel, n_dom, n_rep, inv_scale), out_sh...  45.7 us
    unnamed x11, local copies, waits for them, and re-layouts  5.9 us

profile of v1, /device:TPU:1, one launch (start us, length us, event | category | flops | bytes accessed | tf_op | source)
XLA Modules:
  0.0 52.2 jit_solution(1779407936107406041)
XLA Ops:
  0.6 0.8 %copy.7.columns_ref = s32[1,16,2]{2,1,0:T(8,128)S(1)} copy(s32[1,16,2]{1,2,0:T(2,128)} %param.7) | data formatting | bytes 256 | tf_op args[2]
  1.4 0.0 copy-start
  1.4 1.2 %copy-done = bf16[1,16,2,128,128]{4,3,2,1,0:T(8,128)(2,1)S(1)} copy-done((bf16[1,16,2,128,128]{4,3,2,1,0:T(8,128)(2,1)S(1)}, bf16[1,16,2,128,128]{4,3,2,1,0:T(8,128)(2,1)}, u32[]{:S(2)}) %copy-start) | copy-done | bytes 1048600
  2.6 0.0 copy-start.1
  2.6 0.9 %copy-done.1 = bf16[256,256]{1,0:T(8,128)(2,1)S(1)} copy-done((bf16[256,256]{1,0:T(8,128)(2,1)S(1)}, bf16[256,256]{1,0:T(8,128)(2,1)}, u32[]{:S(2)}) %copy-start.1) | copy-done | bytes 131096
  3.5 0.0 copy-start.2
  3.5 0.8 %copy-done.2 = bf16[128,256]{1,0:T(8,128)(2,1)S(1)} copy-done((bf16[128,256]{1,0:T(8,128)(2,1)S(1)}, bf16[128,256]{1,0:T(8,128)(2,1)}, u32[]{:S(2)}) %copy-start.2) | copy-done | bytes 65560
  4.4 0.0 copy-start.3
  4.4 0.8 %copy-done.3 = bf16[128,256]{1,0:T(8,128)(2,1)S(1)} copy-done((bf16[128,256]{1,0:T(8,128)(2,1)S(1)}, bf16[128,256]{1,0:T(8,128)(2,1)}, u32[]{:S(2)}) %copy-start.3) | copy-done | bytes 65560
  5.2 45.7 %shard_map.68 = (bf16[128,256]{1,0:T(8,128)(2,1)S(1)}, f32[256,256]{1,0:T(8,128)S(1)}) custom-call(s32[1,16,2]{2,1,0:T(8,128)S(1)} %copy.7.columns_ref, bf16[128,256]{1,0:T(8,128)(2,1)S(1)} %copy-done.2, bf16[1,16,2,128,128]{4,3,2,1,0:T(8,128)(2,1)S(1)} %copy-done, bf16[256,256]{1,0:T(8,128)(2,1)S(1)} %copy-done.1, bf16[128,256]{1,0:T(8,128)(2,1)S(1)} %copy-done.3), custom_call_target="tpu_custom_call" | custom-call | tf_op jit(solution)/shard_map/pallas_call | solution.py:256
  50.9 0.6 %copy.10 = bf16[128,256]{1,0:T(8,128)(2,1)} copy(bf16[128,256]{1,0:T(8,128)(2,1)S(1)} %get-tuple-element.4) | data formatting | bytes 131072
  51.5 0.7 %copy.11 = f32[256,256]{1,0:T(8,128)} copy(f32[256,256]{1,0:T(8,128)S(1)} %get-tuple-element.5) | data formatting | bytes 524288
Async XLA Ops:
  1.4 1.2 %copy-start = (bf16[1,16,2,128,128]{4,3,2,1,0:T(8,128)(2,1)S(1)}, bf16[1,16,2,128,128]{4,3,2,1,0:T(8,128)(2,1)}, u32[]{:S(2)}) copy-start(bf16[1,16,2,128,128]{4,3,2,1,0:T(8,128)(2,1)} %values_hbm.1) | copy-start | bytes 3145732
  2.6 0.9 %copy-start.1 = (bf16[256,256]{1,0:T(8,128)(2,1)S(1)}, bf16[256,256]{1,0:T(8,128)(2,1)}, u32[]{:S(2)}) copy-start(bf16[256,256]{1,0:T(8,128)(2,1)} %weight_ref.1) | copy-start | bytes 393220
  3.5 0.8 %copy-start.2 = (bf16[128,256]{1,0:T(8,128)(2,1)S(1)}, bf16[128,256]{1,0:T(8,128)(2,1)}, u32[]{:S(2)}) copy-start(bf16[128,256]{1,0:T(8,128)(2,1)} %features_ref.1) | copy-start | bytes 196612
  4.4 0.8 %copy-start.3 = (bf16[128,256]{1,0:T(8,128)(2,1)S(1)}, bf16[128,256]{1,0:T(8,128)(2,1)}, u32[]{:S(2)}) copy-start(bf16[128,256]{1,0:T(8,128)(2,1)} %cotangent_ref.1) | copy-start | bytes 196612

commit v2 on v1

v2 whole, which is shorter than its diff:
```python
import functools
import math

import jax
import jax.numpy as jnp
from jax import lax
from jax.experimental import pallas as pl
from jax.experimental.pallas import tpu as pltpu
from jax.sharding import PartitionSpec as P

MESH = pl.DeviceIdType.MESH
FACE = 4
SUBLANES = 16
LANES = 128
CHUNKS = 2
VMEM_BYTES = 60 * 1024 * 1024


def flip(index, offset):
    result, bit = index, 1
    while bit <= offset:
        if offset & bit:
            result = result + bit - 2 * bit * ((index // bit) % 2)
        bit *= 2
    return result


def silu_slope(pre_act):
    sigmoid_value = jax.nn.sigmoid(pre_act)
    return sigmoid_value * (1.0 + pre_act * (1.0 - sigmoid_value))


class Sends:
    def __init__(self):
        self.started = []

    def start(self, src, dst, send_sem, recv_sem, target, cond=None):
        def make():
            return pltpu.make_async_remote_copy(
                src_ref=src, dst_ref=dst, send_sem=send_sem, recv_sem=recv_sem,
                device_id=target, device_id_type=MESH,
            )

        when(cond, lambda: make().start())
        self.started.append((cond, make))

    def finish(self):
        for cond, make in self.started:
            when(cond, lambda make=make: make().wait_send())


def when(cond, action):
    if cond is None:
        action()
    else:
        pl.when(cond)(action)


def arrived(ref, send_sem, recv_sem, target):
    pltpu.make_async_remote_copy(
        src_ref=ref, dst_ref=ref, send_sem=send_sem, recv_sem=recv_sem,
        device_id=target, device_id_type=MESH,
    ).wait_recv()


def kernel(
    n_dom, n_rep, inv_scale,
    columns_ref, features_hbm, values_hbm, weight_hbm, cotangent_hbm,
    feature_grad_ref, weight_grad_ref,
    values_ref, weight_ref, cotangent_ref, panels, grad_panels, part_out, part_in,
    weight_part, weight_in1, weight_sum1, weight_in2, weight_sum2, weight_in3, weight_out,
    local_sem, line_send, line_recv, full_send, full_recv, half_send, half_recv,
    part_send, part_recv, weight_send, weight_recv,
):
    rows = cotangent_ref.shape[0]
    rounds = values_ref.shape[0]
    line = n_dom // FACE
    dom, rep = lax.axis_index("dom"), lax.axis_index("rep")
    z, face = dom // FACE, dom % FACE

    def panel_at(z_at, face_at):
        return z_at * FACE + face_at

    line_ids = [panel_at(flip(z, k), face) for k in range(line)]
    face_ids = [panel_at(z, flip(face, j)) for j in range(FACE)]
    rep_ids = [lax.rem(rep + k, n_rep) for k in range(n_rep)]
    from_rep_ids = [lax.rem(rep - k + n_rep, n_rep) for k in range(n_rep)]
    line_to = [{"dom": i} for i in line_ids]
    face_to = [{"dom": i} for i in face_ids]
    rep_to = [{"rep": i} for i in rep_ids]

    local = [
        pltpu.make_async_copy(src, dst, local_sem.at[i])
        for i, (src, dst) in enumerate((
            (features_hbm, panels.at[dom]),
            (values_hbm.at[0], values_ref),
            (weight_hbm, weight_ref),
            (cotangent_hbm, cotangent_ref),
        ))
    ]
    for copy in local:
        copy.start()

    barrier = pltpu.get_barrier_semaphore()
    partners = line_to[1:] + face_to[1:] + rep_to[1:]
    for target in partners:
        pl.semaphore_signal(barrier, inc=1, device_id=target, device_id_type=MESH)
    local[0].wait()
    pl.semaphore_wait(barrier, len(partners))

    sends = Sends()
    chunk = rows // CHUNKS
    half = chunk // 2

    def gather(which, held):
        def source(way, s):
            at = 0 if s == 0 else 1 + 2 * (s - 1) + way
            z_at = z - s if way == 0 else z + s
            if s == 0:
                here = None
            else:
                here = z >= s if way == 0 else z + s < line
            return at, z_at, here

        def sources(s):
            return [source(way, s) for way in range(1 if s == 0 else 2)]

        def rows_of(c):
            return pl.ds(c * chunk, chunk)

        def half_of(c, way):
            return pl.ds(c * chunk + way * half, half)

        def both(first, second):
            return second if first is None else jnp.logical_and(first, second)

        def along(way, s, c):
            at, z_at, here = source(way, s)
            onward = z + 1 < line if way == 0 else z >= 1
            piece = held.at[panel_at(z_at, face), rows_of(c)]
            slot = (which, way, s, c)
            target = {"dom": dom + FACE if way == 0 else dom - FACE}
            sends.start(piece, piece, line_send.at[slot], line_recv.at[slot], target, both(here, onward))

        def to_neighbours(found, c):
            at, z_at, here = found
            piece = held.at[panel_at(z_at, face), rows_of(c)]
            for way in range(2):
                slot = (which, way, at, c)
                sends.start(piece, piece, full_send.at[slot], full_recv.at[slot], face_to[way + 1], here)

        def to_diagonal(s, c):
            for at, z_at, here in sources(s):
                for way in range(2):
                    panel = panel_at(z_at, flip(face, way + 1))
                    slot = (which, way, at, c)
                    piece = held.at[panel, rows_of(c)]
                    when(here, lambda piece=piece, slot=slot, way=way: arrived(
                        piece, full_send.at[slot], full_recv.at[slot], face_to[way + 1]))
                    piece = held.at[panel, half_of(c, way)]
                    slot = (which, 1 - way, at, c)
                    sends.start(piece, piece, half_send.at[slot], half_recv.at[slot], face_to[2 - way], here)

        def begin():
            for c in range(CHUNKS):
                for way in range(2):
                    along(way, 0, c)
                to_neighbours(source(0, 0), c)

        def middle(s):
            for c in range(CHUNKS):
                for way in range(2):
                    found = source(way, s)
                    piece = held.at[panel_at(found[1], face), rows_of(c)]
                    slot = (which, way, s - 1, c)
                    when(found[2], lambda piece=piece, slot=slot: arrived(
                        piece, line_send.at[slot], line_recv.at[slot], {"dom": dom}))
                    if s + 1 < line:
                        along(way, s, c)
                    to_neighbours(found, c)
                to_diagonal(s - 1, c)

        def last():
            for c in range(CHUNKS):
                to_diagonal(line - 1, c)

        def finish():
            for s in range(line):
                for at, z_at, here in sources(s):
                    for c in range(CHUNKS):
                        for way in range(2):
                            piece = held.at[panel_at(z_at, flip(face, 3)), half_of(c, 1 - way)]
                            slot = (which, way, at, c)
                            when(here, lambda piece=piece, slot=slot, way=way: arrived(
                                piece, half_send.at[slot], half_recv.at[slot], face_to[way + 1]))

        steps = [begin]
        steps += [functools.partial(middle, s) for s in range(1, line)]
        steps += [last, finish]
        return steps

    def block_product(held, a):
        left = jnp.concatenate([values_ref[t, a] for t in range(rounds)], axis=1)
        right = jnp.concatenate([held[columns_ref[0, a, t]] for t in range(rounds)], axis=0)
        return jnp.dot(left, right, preferred_element_type=jnp.float32)

    def panel_start(which, held):
        for k in range(1, n_rep):
            part_out[which, k - 1] = block_product(held, rep_ids[k])
            sends.start(
                part_out.at[which, k - 1], part_in.at[which, k - 1],
                part_send.at[which, k - 1], part_recv.at[which, k - 1], rep_to[k],
            )
        return block_product(held, rep)

    def panel_end(which, total):
        for k in range(1, n_rep):
            arrived(
                part_in.at[which, k - 1], part_send.at[which, k - 1],
                part_recv.at[which, k - 1], rep_to[k],
            )
            total = total + part_in[which, k - 1]
        return total.astype(jnp.bfloat16)

    for step in gather(0, panels):
        step()
    for copy in local[1:]:
        copy.wait()
    hidden = panel_end(0, panel_start(0, panels))

    weight = weight_ref[...]
    pre_act = jnp.dot(hidden, weight, preferred_element_type=jnp.float32)
    grad_pre = (cotangent_ref[...].astype(jnp.float32) * silu_slope(pre_act)).astype(jnp.bfloat16)
    grad_panels[dom] = lax.dot_general(
        grad_pre, weight, (((1,), (1,)), ((), ())), preferred_element_type=jnp.float32
    ).astype(jnp.bfloat16)
    back = gather(1, grad_panels)
    back[0]()

    wide = weight.shape[0]
    rep_rows = wide // n_rep
    line_rows = rep_rows // line
    face_rows, face_columns = line_rows // 2, wide // 2
    rep_base = rep * rep_rows
    line_base = rep_base + z * line_rows
    sem_at = [0]

    def weight_sems(count):
        base = sem_at[0]
        sem_at[0] += count - 1
        return [(weight_send.at[base + k - 1], weight_recv.at[base + k - 1]) for k in range(1, count)]

    def span(start, size):
        return (pl.ds(pl.multiple_of(start, SUBLANES), size),)

    def tile(start, f):
        return (
            pl.ds(pl.multiple_of(start + (f // 2) * face_rows, SUBLANES), face_rows),
            pl.ds(pl.multiple_of((f % 2) * face_columns, LANES), face_columns),
        )

    def exchange(out_ref, in_ref, targets, pieces):
        sems = weight_sems(len(targets))
        for k in range(1, len(targets)):
            sends.start(out_ref.at[pieces[k]], in_ref.at[k - 1], *sems[k - 1], targets[k])
        return sems

    def take(in_ref, sems, targets, total):
        for k in range(1, len(targets)):
            arrived(in_ref.at[k - 1], *sems[k - 1], targets[k])
            total = total + in_ref[k - 1]
        return total

    def share(piece, targets):
        sems = weight_sems(len(targets))
        for k in range(1, len(targets)):
            sends.start(weight_out.at[piece], weight_out.at[piece], *sems[k - 1], targets[k])
        return sems

    def collect(pieces, sems, targets):
        for k in range(1, len(targets)):
            arrived(weight_out.at[pieces[k]], *sems[k - 1], targets[k])

    line_z = [flip(z, k) for k in range(line)]
    face_f = [flip(face, j) for j in range(FACE)]

    weight_part[...] = lax.dot_general(
        hidden, grad_pre, (((0,), (0,)), ((), ())), preferred_element_type=jnp.float32
    )
    sems1 = exchange(weight_part, weight_in1, rep_to, [span(i * rep_rows, rep_rows) for i in rep_ids])
    back[1]()
    weight_sum1[...] = take(weight_in1, sems1, rep_to, weight_part[span(rep_base, rep_rows)])
    sems2 = exchange(weight_sum1, weight_in2, line_to, [span(i * line_rows, line_rows) for i in line_z])
    for step in back[2:line]:
        step()
    weight_sum2[...] = take(weight_in2, sems2, line_to, weight_sum1[span(z * line_rows, line_rows)])
    sems3 = exchange(weight_sum2, weight_in3, face_to, [tile(0, f) for f in face_f])
    back[line]()
    own_sum = take(weight_in3, sems3, face_to, weight_sum2[tile(0, face)])
    weight_out[tile(line_base, face)] = (own_sum * inv_scale).astype(jnp.bfloat16)
    sems4 = share(tile(line_base, face), face_to)
    back[line + 1]()
    collect([tile(line_base, f) for f in face_f], sems4, face_to)
    sems5 = share(span(line_base, line_rows), line_to)

    total = panel_start(1, grad_panels)
    collect([span(rep_base + i * line_rows, line_rows) for i in line_z], sems5, line_to)
    sems6 = share(span(rep_base, rep_rows), rep_to)
    feature_grad_ref[...] = panel_end(1, total)
    collect([span(i * rep_rows, rep_rows) for i in from_rep_ids], sems6, rep_to)
    weight_grad_ref[...] = weight_out[...]
    sends.finish()


def kernel_shards(features, block_values, block_columns, weight, cotangent):
    n_dom, n_rep = lax.axis_size("dom"), lax.axis_size("rep")
    rows, width = features.shape
    wide = weight.shape[0]
    line = n_dom // FACE
    rep_rows = wide // n_rep
    line_rows = rep_rows // line
    inv_scale = 1.0 / math.sqrt(rows * n_dom * n_rep)
    weight_copies = 2 * ((n_rep - 1) + (line - 1) + (FACE - 1))
    parts, steps = max(n_rep - 1, 1), max(line - 1, 1)
    vmem = pl.BlockSpec(memory_space=pltpu.VMEM)
    any_space = pl.BlockSpec(memory_space=pl.ANY)
    dma = pltpu.SemaphoreType.DMA
    face_slots = (2, 2, 2 * line - 1, CHUNKS)
    line_slots = (2, 2, steps, CHUNKS)
    feature_grad, weight_grad = pl.pallas_call(
        functools.partial(kernel, n_dom, n_rep, inv_scale),
        out_shape=(
            jax.ShapeDtypeStruct((rows, width), jnp.bfloat16),
            jax.ShapeDtypeStruct(weight.shape, jnp.bfloat16),
        ),
        in_specs=[pl.BlockSpec(memory_space=pltpu.SMEM)] + [any_space] * 4,
        out_specs=(vmem, vmem),
        scratch_shapes=[
            pltpu.VMEM(block_values.shape[1:], jnp.bfloat16),
            pltpu.VMEM(weight.shape, jnp.bfloat16),
            pltpu.VMEM(cotangent.shape, jnp.bfloat16),
            pltpu.VMEM((n_dom, rows, width), jnp.bfloat16),
            pltpu.VMEM((n_dom, rows, width), jnp.bfloat16),
            pltpu.VMEM((2, parts, rows, width), jnp.float32),
            pltpu.VMEM((2, parts, rows, width), jnp.float32),
            pltpu.VMEM(weight.shape, jnp.float32),
            pltpu.VMEM((parts, rep_rows, wide), jnp.float32),
            pltpu.VMEM((rep_rows, wide), jnp.float32),
            pltpu.VMEM((steps, line_rows, wide), jnp.float32),
            pltpu.VMEM((line_rows, wide), jnp.float32),
            pltpu.VMEM((FACE - 1, line_rows // 2, wide // 2), jnp.float32),
            pltpu.VMEM(weight.shape, jnp.bfloat16),
            dma((4,)),
            dma(line_slots), dma(line_slots),
            dma(face_slots), dma(face_slots),
            dma(face_slots), dma(face_slots),
            dma((2, parts)), dma((2, parts)),
            dma((weight_copies,)), dma((weight_copies,)),
        ],
        compiler_params=pltpu.CompilerParams(
            collective_id=0, has_side_effects=True, vmem_limit_bytes=VMEM_BYTES
        ),
    )(jnp.swapaxes(block_columns, 1, 2), features, block_values, weight, cotangent)
    return feature_grad, weight_grad.astype(jnp.float32)


def panel_product(values, columns, gathered, block_rows):
    panel_count = gathered.shape[0] // block_rows
    panels = gathered.reshape(panel_count, block_rows, gathered.shape[1])
    picked = panels[columns]
    summed = jnp.einsum("taij,tajf->aif", values, picked, preferred_element_type=jnp.float32)
    return summed.reshape(-1, summed.shape[-1])


def plain_shards(features, block_values, block_columns, weight, cotangent):
    block_rows = features.shape[0]
    values, columns = block_values[0], block_columns[0]
    gathered = lax.all_gather(features, "dom", axis=0, tiled=True)
    inv_scale = 1.0 / math.sqrt(gathered.shape[0] * lax.axis_size("rep"))
    partial_value = panel_product(values, columns, gathered, block_rows)
    hidden = lax.psum_scatter(partial_value, "rep", scatter_dimension=0, tiled=True).astype(jnp.bfloat16)
    pre_act = jnp.dot(hidden, weight, preferred_element_type=jnp.float32)
    grad_pre = (cotangent.astype(jnp.float32) * silu_slope(pre_act)).astype(jnp.bfloat16)
    hidden_grad = jnp.einsum(
        "rg,fg->rf", grad_pre, weight, preferred_element_type=jnp.float32
    ).astype(jnp.bfloat16)
    weight_part = jnp.einsum("rf,rg->fg", hidden, grad_pre, preferred_element_type=jnp.float32)
    weight_grad = lax.psum(weight_part, ("dom", "rep")) * inv_scale
    grad_rows = lax.all_gather(hidden_grad, "dom", axis=0, tiled=True)
    back_partial = panel_product(values, columns, grad_rows, block_rows)
    feature_grad = lax.psum_scatter(back_partial, "rep", scatter_dimension=0, tiled=True)
    return (feature_grad.astype(jnp.bfloat16), weight_grad)


def shards(features, block_values, block_columns, weight, cotangent):
    n_dom, n_rep = lax.axis_size("dom"), lax.axis_size("rep")
    line = n_dom // FACE
    splits = (
        n_dom % FACE == 0
        and line & (line - 1) == 0
        and weight.shape[0] % (2 * SUBLANES * line * n_rep) == 0
        and weight.shape[0] % (2 * LANES) == 0
        and features.shape[0] % (2 * SUBLANES * CHUNKS) == 0
    )
    body = kernel_shards if splits else plain_shards
    return body(features, block_values, block_columns, weight, cotangent)


def solution(mesh):
    return jax.shard_map(
        shards,
        mesh=mesh,
        in_specs=(
            P(("dom", "rep"), None),
            P(("dom", "rep"), None, None, None, None),
            P(("dom", "rep"), None, None),
            P(),
            P(("dom", "rep"), None),
        ),
        out_specs=(P(("dom", "rep"), None), P()),
        check_vma=False,
    )
```

time: 52.5 us -> 52.8 us (level)
  local copies, waits for them, and re-layouts: 5.9 us -> 0.63 us
  Pallas kernels: 45.7 us -> 49.7 us
  other arithmetic: 0 us -> 1.66 us
    unnamed x11 -> x3, local copies, waits for them, and re-layouts: 5.9 us -> 0.63 us
    pallas_call x1, Pallas kernels: 45.7 us -> 49.7 us  [kernel_shards(): pl.pallas_call(functools.partial(kernel, n_dom, n_rep, inv_scale), out_sh...]
    convert_element_type x0 -> x1, other arithmetic: none -> 1.66 us  [kernel_shards(): return (feature_grad, weight_grad.astype(jnp.float32))]
where the time goes in v2:
time: 52.8 us; the launch traced here: 52.6 us
  Pallas kernels  49.7 us (94%)
  other arithmetic  1.66 us (3%)
  between operations  0.65 us (1%)
  local copies, waits for them, and re-layouts  0.63 us (1%)
    pallas_call x1, Pallas kernels, kernel_shards(): pl.pallas_call(functools.partial(kernel, n_dom, n_rep, inv_scale), out_sh...  49.7 us
    convert_element_type x1, other arithmetic, kernel_shards(): return (feature_grad, weight_grad.astype(jnp.float32))  1.66 us

profile of v2, /device:TPU:1, one launch (start us, length us, event | category | flops | bytes accessed | tf_op | source)
XLA Modules:
  0.0 52.6 jit_solution(2717636881420467508)
XLA Ops:
  0.6 49.7 %shard_map.68 = (bf16[128,256]{1,0:T(8,128)(2,1)}, bf16[256,256]{1,0:T(8,128)(2,1)}) custom-call(s32[1,2,16]{2,1,0:T(2,128)} %bitcast.1, bf16[128,256]{1,0:T(8,128)(2,1)} %features_hbm.1, bf16[1,16,2,128,128]{4,3,2,1,0:T(8,128)(2,1)} %values_hbm.1, bf16[256,256]{1,0:T(8,128)(2,1)} %weight_hbm.1, bf16[128,256]{1,0:T(8,128)(2,1)} %cotangent_hbm.1), custom_call_target="tpu_custom_call" | custom-call | tf_op jit(solution)/shard_map/pallas_call | solution.py:330
  50.3 0.0 copy-start
  50.4 1.7 %convert_element_type.3 = f32[256,256]{1,0:T(8,128)} convert(bf16[256,256]{1,0:T(8,128)(2,1)} %get-tuple-element.5) | non-fusion elementwise | flops 65536 | bytes 393216 | tf_op jit(solution)/shard_map/convert_element_type | solution.py:364
  52.0 0.0 copy-done
  52.0 0.6 %copy.8 = bf16[128,256]{1,0:T(8,128)(2,1)} copy(bf16[128,256]{1,0:T(8,128)(2,1)S(1)} %copy-done) | data formatting | bytes 131072
Async XLA Ops:
  50.3 1.7 %copy-start = (bf16[128,256]{1,0:T(8,128)(2,1)S(1)}, bf16[128,256]{1,0:T(8,128)(2,1)}, u32[]{:S(2)}) copy-start(bf16[128,256]{1,0:T(8,128)(2,1)} %get-tuple-element.8) | copy-start | bytes 196612

commit v3 on v2

--- a/solution.py
+++ b/solution.py
@@ -12,7 +12,6 @@
 FACE = 4
 SUBLANES = 16
 LANES = 128
-CHUNKS = 2
 VMEM_BYTES = 60 * 1024 * 1024
 
 
@@ -34,26 +33,22 @@
     def __init__(self):
         self.started = []
 
-    def start(self, src, dst, send_sem, recv_sem, target, cond=None):
-        def make():
-            return pltpu.make_async_remote_copy(
-                src_ref=src, dst_ref=dst, send_sem=send_sem, recv_sem=recv_sem,
-                device_id=target, device_id_type=MESH,
-            )
-
-        when(cond, lambda: make().start())
-        self.started.append((cond, make))
+    def start(self, src, dst, send_sem, recv_sem, target):
+        copy = pltpu.make_async_remote_copy(
+            src_ref=src, dst_ref=dst, send_sem=send_sem, recv_sem=recv_sem,
+            device_id=target, device_id_type=MESH,
+        )
+        copy.start()
+        self.started.append(copy)
+        return copy
+
+    def left(self, copy):
+        copy.wait_send()
+        self.started = [other for other in self.started if other is not copy]
 
     def finish(self):
-        for cond, make in self.started:
-            when(cond, lambda make=make: make().wait_send())
-
-
-def when(cond, action):
-    if cond is None:
-        action()
-    else:
-        pl.when(cond)(action)
+        for copy in self.started:
+            copy.wait_send()
 
 
 def arrived(ref, send_sem, recv_sem, target):
@@ -109,93 +104,68 @@
     pl.semaphore_wait(barrier, len(partners))
 
     sends = Sends()
-    chunk = rows // CHUNKS
-    half = chunk // 2
+    half = rows // 2
 
     def gather(which, held):
-        def source(way, s):
-            at = 0 if s == 0 else 1 + 2 * (s - 1) + way
-            z_at = z - s if way == 0 else z + s
-            if s == 0:
-                here = None
-            else:
-                here = z >= s if way == 0 else z + s < line
-            return at, z_at, here
-
-        def sources(s):
-            return [source(way, s) for way in range(1 if s == 0 else 2)]
-
-        def rows_of(c):
-            return pl.ds(c * chunk, chunk)
-
-        def half_of(c, way):
-            return pl.ds(c * chunk + way * half, half)
-
-        def both(first, second):
-            return second if first is None else jnp.logical_and(first, second)
-
-        def along(way, s, c):
-            at, z_at, here = source(way, s)
-            onward = z + 1 < line if way == 0 else z >= 1
-            piece = held.at[panel_at(z_at, face), rows_of(c)]
-            slot = (which, way, s, c)
-            target = {"dom": dom + FACE if way == 0 else dom - FACE}
-            sends.start(piece, piece, line_send.at[slot], line_recv.at[slot], target, both(here, onward))
-
-        def to_neighbours(found, c):
-            at, z_at, here = found
-            piece = held.at[panel_at(z_at, face), rows_of(c)]
+        halves = (pl.ds(0, half), pl.ds(half, half))
+
+        def along(k):
+            own = held.at[dom]
+            return sends.start(own, own, line_send.at[which, k - 1], line_recv.at[which, k - 1], line_to[k])
+
+        def next_along(k):
+            if k < line:
+                sends.left(pending.pop())
+                pending.append(along(k))
+
+        pending = []
+
+        def to_neighbours(k):
+            piece = held.at[line_ids[k]]
             for way in range(2):
-                slot = (which, way, at, c)
-                sends.start(piece, piece, full_send.at[slot], full_recv.at[slot], face_to[way + 1], here)
-
-        def to_diagonal(s, c):
-            for at, z_at, here in sources(s):
+                slot = (which, way, k)
+                sends.start(piece, piece, full_send.at[slot], full_recv.at[slot], face_to[way + 1])
+
+        def to_diagonal(k):
+            for way in range(2):
+                panel = panel_at(flip(z, k), flip(face, way + 1))
+                slot = (which, way, k)
+                arrived(held.at[panel], full_send.at[slot], full_recv.at[slot], face_to[way + 1])
+                piece = held.at[panel, halves[way]]
+                slot = (which, 1 - way, k)
+                sends.start(piece, piece, half_send.at[slot], half_recv.at[slot], face_to[2 - way])
+
+        def begin():
+            if line > 1:
+                pending.append(along(1))
+            to_neighbours(0)
+
+        def own_diagonal():
+            next_along(2)
+            to_diagonal(0)
+
+        def middle(k):
+            arrived(held.at[line_ids[k]], line_send.at[which, k - 1], line_recv.at[which, k - 1], line_to[k])
+            to_neighbours(k)
+            next_along(k + 2)
+            if k > 1:
+                to_diagonal(k - 1)
+
+        def last():
+            if line > 1:
+                to_diagonal(line - 1)
+
+        def finish():
+            for k in range(line):
+                panel = panel_at(flip(z, k), flip(face, 3))
                 for way in range(2):
-                    panel = panel_at(z_at, flip(face, way + 1))
-                    slot = (which, way, at, c)
-                    piece = held.at[panel, rows_of(c)]
-                    when(here, lambda piece=piece, slot=slot, way=way: arrived(
-                        piece, full_send.at[slot], full_recv.at[slot], face_to[way + 1]))
-                    piece = held.at[panel, half_of(c, way)]
-                    slot = (which, 1 - way, at, c)
-                    sends.start(piece, piece, half_send.at[slot], half_recv.at[slot], face_to[2 - way], here)
-
-        def begin():
-            for c in range(CHUNKS):
-                for way in range(2):
-                    along(way, 0, c)
-                to_neighbours(source(0, 0), c)
-
-        def middle(s):
-            for c in range(CHUNKS):
-                for way in range(2):
-                    found = source(way, s)
-                    piece = held.at[panel_at(found[1], face), rows_of(c)]
-                    slot = (which, way, s - 1, c)
-                    when(found[2], lambda piece=piece, slot=slot: arrived(
-                        piece, line_send.at[slot], line_recv.at[slot], {"dom": dom}))
-                    if s + 1 < line:
-                        along(way, s, c)
-                    to_neighbours(found, c)
-                to_diagonal(s - 1, c)
-
-        def last():
-            for c in range(CHUNKS):
-                to_diagonal(line - 1, c)
-
-        def finish():
-            for s in range(line):
-                for at, z_at, here in sources(s):
-                    for c in range(CHUNKS):
-                        for way in range(2):
-                            piece = held.at[panel_at(z_at, flip(face, 3)), half_of(c, 1 - way)]
-                            slot = (which, way, at, c)
-                            when(here, lambda piece=piece, slot=slot, way=way: arrived(
-                                piece, half_send.at[slot], half_recv.at[slot], face_to[way + 1]))
-
-        steps = [begin]
-        steps += [functools.partial(middle, s) for s in range(1, line)]
+                    slot = (which, way, k)
+                    arrived(
+                        held.at[panel, halves[1 - way]], half_send.at[slot], half_recv.at[slot], face_to[way + 1]
+                    )
+
+        steps = [begin, own_diagonal]
+        steps += [functools.partial(middle, k) for k in range(1, line)]
         steps += [last, finish]
         return steps
 
@@ -289,17 +259,18 @@
     )
     sems1 = exchange(weight_part, weight_in1, rep_to, [span(i * rep_rows, rep_rows) for i in rep_ids])
     back[1]()
+    back[2]()
     weight_sum1[...] = take(weight_in1, sems1, rep_to, weight_part[span(rep_base, rep_rows)])
     sems2 = exchange(weight_sum1, weight_in2, line_to, [span(i * line_rows, line_rows) for i in line_z])
-    for step in back[2:line]:
+    for step in back[3:-2]:
         step()
     weight_sum2[...] = take(weight_in2, sems2, line_to, weight_sum1[span(z * line_rows, line_rows)])
     sems3 = exchange(weight_sum2, weight_in3, face_to, [tile(0, f) for f in face_f])
-    back[line]()
+    back[-2]()
     own_sum = take(weight_in3, sems3, face_to, weight_sum2[tile(0, face)])
     weight_out[tile(line_base, face)] = (own_sum * inv_scale).astype(jnp.bfloat16)
     sems4 = share(tile(line_base, face), face_to)
-    back[line + 1]()
+    back[-1]()
     collect([tile(line_base, f) for f in face_f], sems4, face_to)
     sems5 = share(span(line_base, line_rows), line_to)
 
@@ -325,8 +296,8 @@
     vmem = pl.BlockSpec(memory_space=pltpu.VMEM)
     any_space = pl.BlockSpec(memory_space=pl.ANY)
     dma = pltpu.SemaphoreType.DMA
-    face_slots = (2, 2, 2 * line - 1, CHUNKS)
-    line_slots = (2, 2, steps, CHUNKS)
+    face_slots = (2, 2, line)
+    line_slots = (2, steps)
     feature_grad, weight_grad = pl.pallas_call(
         functools.partial(kernel, n_dom, n_rep, inv_scale),
         out_shape=(
@@ -400,7 +371,7 @@
         and line & (line - 1) == 0
         and weight.shape[0] % (2 * SUBLANES * line * n_rep) == 0
         and weight.shape[0] % (2 * LANES) == 0
-        and features.shape[0] % (2 * SUBLANES * CHUNKS) == 0
+        and features.shape[0] % (2 * SUBLANES) == 0
     )
     body = kernel_shards if splits else plain_shards
     return body(features, block_values, block_columns, weight, cotangent)

time: 52.8 us -> 53.6 us (1.015)
  Pallas kernels: 49.7 us -> 50.5 us
    pallas_call x1, Pallas kernels: 49.7 us -> 50.5 us  [kernel_shards(): pl.pallas_call(functools.partial(kernel, n_dom, n_rep, inv_scale), out_sh...]
where the time goes in v3:
time: 53.6 us; the launch traced here: 53.4 us
  Pallas kernels  50.5 us (94%)
  other arithmetic  1.66 us (3%)
  between operations  0.65 us (1%)
  local copies, waits for them, and re-layouts  0.63 us (1%)
    pallas_call x1, Pallas kernels, kernel_shards(): pl.pallas_call(functools.partial(kernel, n_dom, n_rep, inv_scale), out_sh...  50.5 us
    convert_element_type x1, other arithmetic, kernel_shards(): return (feature_grad, weight_grad.astype(jnp.float32))  1.66 us

profile of v3, /device:TPU:1, one launch (start us, length us, event | category | flops | bytes accessed | tf_op | source)
XLA Modules:
  0.0 53.4 jit_solution(17854879616695100492)
XLA Ops:
  0.6 50.5 %shard_map.68 = (bf16[128,256]{1,0:T(8,128)(2,1)}, bf16[256,256]{1,0:T(8,128)(2,1)}) custom-call(s32[1,2,16]{2,1,0:T(2,128)} %bitcast.1, bf16[128,256]{1,0:T(8,128)(2,1)} %features_hbm.1, bf16[1,16,2,128,128]{4,3,2,1,0:T(8,128)(2,1)} %values_hbm.1, bf16[256,256]{1,0:T(8,128)(2,1)} %weight_hbm.1, bf16[128,256]{1,0:T(8,128)(2,1)} %cotangent_hbm.1), custom_call_target="tpu_custom_call" | custom-call | tf_op jit(solution)/shard_map/pallas_call | solution.py:301
  51.1 0.0 copy-start
  51.1 1.7 %convert_element_type.3 = f32[256,256]{1,0:T(8,128)} convert(bf16[256,256]{1,0:T(8,128)(2,1)} %get-tuple-element.5) | non-fusion elementwise | flops 65536 | bytes 393216 | tf_op jit(solution)/shard_map/convert_element_type | solution.py:335
  52.8 0.0 copy-done
  52.8 0.6 %copy.8 = bf16[128,256]{1,0:T(8,128)(2,1)} copy(bf16[128,256]{1,0:T(8,128)(2,1)S(1)} %copy-done) | data formatting | bytes 131072
Async XLA Ops:
  51.1 1.7 %copy-start = (bf16[128,256]{1,0:T(8,128)(2,1)S(1)}, bf16[128,256]{1,0:T(8,128)(2,1)}, u32[]{:S(2)}) copy-start(bf16[128,256]{1,0:T(8,128)(2,1)} %get-tuple-element.8) | copy-start | bytes 196612

commit v4 on v3

--- a/solution.py
+++ b/solution.py
@@ -40,11 +40,6 @@
         )
         copy.start()
         self.started.append(copy)
-        return copy
-
-    def left(self, copy):
-        copy.wait_send()
-        self.started = [other for other in self.started if other is not copy]
 
     def finish(self):
         for copy in self.started:
@@ -111,14 +106,7 @@
 
         def along(k):
             own = held.at[dom]
-            return sends.start(own, own, line_send.at[which, k - 1], line_recv.at[which, k - 1], line_to[k])
-
-        def next_along(k):
-            if k < line:
-                sends.left(pending.pop())
-                pending.append(along(k))
-
-        pending = []
+            sends.start(own, own, line_send.at[which, k - 1], line_recv.at[which, k - 1], line_to[k])
 
         def to_neighbours(k):
             piece = held.at[line_ids[k]]
@@ -136,18 +124,16 @@
                 sends.start(piece, piece, half_send.at[slot], half_recv.at[slot], face_to[2 - way])
 
         def begin():
-            if line > 1:
-                pending.append(along(1))
+            for k in range(1, line):
+                along(k)
             to_neighbours(0)
 
         def own_diagonal():
-            next_along(2)
             to_diagonal(0)
 
         def middle(k):
             arrived(held.at[line_ids[k]], line_send.at[which, k - 1], line_recv.at[which, k - 1], line_to[k])
             to_neighbours(k)
-            next_along(k + 2)
             if k > 1:
                 to_diagonal(k - 1)
 
@@ -279,7 +265,7 @@
     sems6 = share(span(rep_base, rep_rows), rep_to)
     feature_grad_ref[...] = panel_end(1, total)
     collect([span(i * rep_rows, rep_rows) for i in from_rep_ids], sems6, rep_to)
-    weight_grad_ref[...] = weight_out[...]
+    weight_grad_ref[...] = weight_out[...].astype(jnp.float32)
     sends.finish()
 
 
@@ -294,17 +280,17 @@
     weight_copies = 2 * ((n_rep - 1) + (line - 1) + (FACE - 1))
     parts, steps = max(n_rep - 1, 1), max(line - 1, 1)
     vmem = pl.BlockSpec(memory_space=pltpu.VMEM)
-    any_space = pl.BlockSpec(memory_space=pl.ANY)
+    hbm = pl.BlockSpec(memory_space=pl.ANY)
     dma = pltpu.SemaphoreType.DMA
     face_slots = (2, 2, line)
     line_slots = (2, steps)
-    feature_grad, weight_grad = pl.pallas_call(
+    return pl.pallas_call(
         functools.partial(kernel, n_dom, n_rep, inv_scale),
         out_shape=(
             jax.ShapeDtypeStruct((rows, width), jnp.bfloat16),
-            jax.ShapeDtypeStruct(weight.shape, jnp.bfloat16),
+            jax.ShapeDtypeStruct(weight.shape, jnp.float32),
         ),
-        in_specs=[pl.BlockSpec(memory_space=pltpu.SMEM)] + [any_space] * 4,
+        in_specs=[pl.BlockSpec(memory_space=pltpu.SMEM)] + [hbm] * 4,
         out_specs=(vmem, vmem),
         scratch_shapes=[
             pltpu.VMEM(block_values.shape[1:], jnp.bfloat16),
@@ -332,7 +318,6 @@
             collective_id=0, has_side_effects=True, vmem_limit_bytes=VMEM_BYTES
         ),
     )(jnp.swapaxes(block_columns, 1, 2), features, block_values, weight, cotangent)
-    return feature_grad, weight_grad.astype(jnp.float32)
 
 
 def panel_product(values, columns, gathered, block_rows):

time: 53.6 us -> 49.5 us (0.924)
  Pallas kernels: 50.5 us -> 45.5 us
  local copies, waits for them, and re-layouts: 0.63 us -> 3.14 us
  other arithmetic: 1.66 us -> 0 us
    pallas_call x1, Pallas kernels: 50.5 us -> 45.5 us  [kernel_shards(): pl.pallas_call(functools.partial(kernel, n_dom, n_rep, inv_scale), out_sh...]
    unnamed x3 -> x2, local copies, waits for them, and re-layouts: 0.63 us -> 3.14 us
    convert_element_type x1 -> x0, other arithmetic: 1.66 us -> none  [kernel_shards(): return (feature_grad, weight_grad.astype(jnp.float32))]
where the time goes in v4:
time: 49.5 us; the launch traced here: 49.3 us
  Pallas kernels  45.5 us (92%)
  local copies, waits for them, and re-layouts  3.14 us (6%)
  between operations  0.64 us (1%)
    pallas_call x1, Pallas kernels, kernel_shards(): pl.pallas_call(functools.partial(kernel, n_dom, n_rep, inv_scale), out_sh...  45.5 us
    unnamed x2, local copies, waits for them, and re-layouts  3.14 us

profile of v4, /device:TPU:1, one launch (start us, length us, event | category | flops | bytes accessed | tf_op | source)
XLA Modules:
  0.0 49.3 jit_solution(12824439533272333794)
XLA Ops:
  0.6 45.5 %shard_map.68 = (bf16[128,256]{1,0:T(8,128)(2,1)}, f32[256,256]{1,0:T(8,128)}) custom-call(s32[1,2,16]{2,1,0:T(2,128)} %bitcast.1, bf16[128,256]{1,0:T(8,128)(2,1)} %features_hbm.1, bf16[1,16,2,128,128]{4,3,2,1,0:T(8,128)(2,1)} %values_hbm.1, bf16[256,256]{1,0:T(8,128)(2,1)} %weight_hbm.1, bf16[128,256]{1,0:T(8,128)(2,1)} %cotangent_hbm.1), custom_call_target="tpu_custom_call" | custom-call | tf_op jit(solution)/shard_map/pallas_call | solution.py:287
  46.2 1.5 %copy.9 = bf16[128,256]{1,0:T(8,128)(2,1)} copy(bf16[128,256]{1,0:T(8,128)(2,1)} %get-tuple-element.4) | data formatting | bytes 131072
  47.6 1.7 %copy.10 = f32[256,256]{1,0:T(8,128)} copy(f32[256,256]{1,0:T(8,128)} %get-tuple-element.5) | data formatting | bytes 524288

commit v5 on v4

--- a/solution.py
+++ b/solution.py
@@ -195,10 +195,10 @@
 
     wide = weight.shape[0]
     rep_rows = wide // n_rep
-    line_rows = rep_rows // line
-    face_rows, face_columns = line_rows // 2, wide // 2
+    face_rows = rep_rows // FACE
+    line_rows, line_columns = 2 * face_rows // line, wide // 2
     rep_base = rep * rep_rows
-    line_base = rep_base + z * line_rows
+    face_base = rep_base + face * face_rows
     sem_at = [0]
 
     def weight_sems(count):
@@ -209,10 +209,10 @@
     def span(start, size):
         return (pl.ds(pl.multiple_of(start, SUBLANES), size),)
 
-    def tile(start, f):
+    def tile(start, z_at):
         return (
-            pl.ds(pl.multiple_of(start + (f // 2) * face_rows, SUBLANES), face_rows),
-            pl.ds(pl.multiple_of((f % 2) * face_columns, LANES), face_columns),
+            pl.ds(pl.multiple_of(start + (z_at // 2) * line_rows, SUBLANES), line_rows),
+            pl.ds(pl.multiple_of((z_at % 2) * line_columns, LANES), line_columns),
         )
 
     def exchange(out_ref, in_ref, targets, pieces):
@@ -245,23 +245,24 @@
     )
     sems1 = exchange(weight_part, weight_in1, rep_to, [span(i * rep_rows, rep_rows) for i in rep_ids])
     back[1]()
-    back[2]()
     weight_sum1[...] = take(weight_in1, sems1, rep_to, weight_part[span(rep_base, rep_rows)])
-    sems2 = exchange(weight_sum1, weight_in2, line_to, [span(i * line_rows, line_rows) for i in line_z])
+    sems2 = exchange(weight_sum1, weight_in2, face_to, [span(f * face_rows, face_rows) for f in face_f])
+    for step in back[2:3]:
+        step()
+    weight_sum2[...] = take(weight_in2, sems2, face_to, weight_sum1[span(face * face_rows, face_rows)])
+    sems3 = exchange(weight_sum2, weight_in3, line_to, [tile(0, i) for i in line_z])
     for step in back[3:-2]:
         step()
-    weight_sum2[...] = take(weight_in2, sems2, line_to, weight_sum1[span(z * line_rows, line_rows)])
-    sems3 = exchange(weight_sum2, weight_in3, face_to, [tile(0, f) for f in face_f])
+    own_sum = take(weight_in3, sems3, line_to, weight_sum2[tile(0, z)])
+    weight_out[tile(face_base, z)] = (own_sum * inv_scale).astype(jnp.bfloat16)
+    sems4 = share(tile(face_base, z), line_to)
     back[-2]()
-    own_sum = take(weight_in3, sems3, face_to, weight_sum2[tile(0, face)])
-    weight_out[tile(line_base, face)] = (own_sum * inv_scale).astype(jnp.bfloat16)
-    sems4 = share(tile(line_base, face), face_to)
+    collect([tile(face_base, i) for i in line_z], sems4, line_to)
+    sems5 = share(span(face_base, face_rows), face_to)
     back[-1]()
-    collect([tile(line_base, f) for f in face_f], sems4, face_to)
-    sems5 = share(span(line_base, line_rows), line_to)
 
     total = panel_start(1, grad_panels)
-    collect([span(rep_base + i * line_rows, line_rows) for i in line_z], sems5, line_to)
+    collect([span(rep_base + f * face_rows, face_rows) for f in face_f], sems5, face_to)
     sems6 = share(span(rep_base, rep_rows), rep_to)
     feature_grad_ref[...] = panel_end(1, total)
     collect([span(i * rep_rows, rep_rows) for i in from_rep_ids], sems6, rep_to)
@@ -275,7 +276,7 @@
     wide = weight.shape[0]
     line = n_dom // FACE
     rep_rows = wide // n_rep
-    line_rows = rep_rows // line
+    face_rows = rep_rows // FACE
     inv_scale = 1.0 / math.sqrt(rows * n_dom * n_rep)
     weight_copies = 2 * ((n_rep - 1) + (line - 1) + (FACE - 1))
     parts, steps = max(n_rep - 1, 1), max(line - 1, 1)
@@ -303,9 +304,9 @@
             pltpu.VMEM(weight.shape, jnp.float32),
             pltpu.VMEM((parts, rep_rows, wide), jnp.float32),
             pltpu.VMEM((rep_rows, wide), jnp.float32),
-            pltpu.VMEM((steps, line_rows, wide), jnp.float32),
-            pltpu.VMEM((line_rows, wide), jnp.float32),
-            pltpu.VMEM((FACE - 1, line_rows // 2, wide // 2), jnp.float32),
+            pltpu.VMEM((FACE - 1, face_rows, wide), jnp.float32),
+            pltpu.VMEM((face_rows, wide), jnp.float32),
+            pltpu.VMEM((steps, 2 * face_rows // line, wide // 2), jnp.float32),
             pltpu.VMEM(weight.shape, jnp.bfloat16),
             dma((4,)),
             dma(line_slots), dma(line_slots),
@@ -354,6 +355,7 @@
     splits = (
         n_dom % FACE == 0
         and line & (line - 1) == 0
+        and line > 1
         and weight.shape[0] % (2 * SUBLANES * line * n_rep) == 0
         and weight.shape[0] % (2 * LANES) == 0
         and features.shape[0] % (2 * SUBLANES) == 0

time: 49.5 us -> 48.1 us (0.972)
  Pallas kernels: 45.5 us -> 44.1 us
    pallas_call x1, Pallas kernels: 45.5 us -> 44.1 us  [kernel_shards(): pl.pallas_call(functools.partial(kernel, n_dom, n_rep, inv_scale), out_sh...]
where the time goes in v5:
time: 48.1 us; the launch traced here: 47.8 us
  Pallas kernels  44.1 us (92%)
  local copies, waits for them, and re-layouts  3.14 us (7%)
  between operations  0.64 us (1%)
    pallas_call x1, Pallas kernels, kernel_shards(): pl.pallas_call(functools.partial(kernel, n_dom, n_rep, inv_scale), out_sh...  44.1 us
    unnamed x2, local copies, waits for them, and re-layouts  3.14 us

profile of v5, /device:TPU:1, one launch (start us, length us, event | category | flops | bytes accessed | tf_op | source)
XLA Modules:
  0.0 47.8 jit_solution(16741805302805351029)
XLA Ops:
  0.6 44.1 %shard_map.68 = (bf16[128,256]{1,0:T(8,128)(2,1)}, f32[256,256]{1,0:T(8,128)}) custom-call(s32[1,2,16]{2,1,0:T(2,128)} %bitcast.1, bf16[128,256]{1,0:T(8,128)(2,1)} %features_hbm.1, bf16[1,16,2,128,128]{4,3,2,1,0:T(8,128)(2,1)} %values_hbm.1, bf16[256,256]{1,0:T(8,128)(2,1)} %weight_hbm.1, bf16[128,256]{1,0:T(8,128)(2,1)} %cotangent_hbm.1), custom_call_target="tpu_custom_call" | custom-call | tf_op jit(solution)/shard_map/pallas_call | solution.py:288
  44.7 1.5 %copy.9 = bf16[128,256]{1,0:T(8,128)(2,1)} copy(bf16[128,256]{1,0:T(8,128)(2,1)} %get-tuple-element.4) | data formatting | bytes 131072
  46.2 1.7 %copy.10 = f32[256,256]{1,0:T(8,128)} copy(f32[256,256]{1,0:T(8,128)} %get-tuple-element.5) | data formatting | bytes 524288

commit v6 on v5

--- a/solution.py
+++ b/solution.py
@@ -288,8 +288,8 @@
     return pl.pallas_call(
         functools.partial(kernel, n_dom, n_rep, inv_scale),
         out_shape=(
-            jax.ShapeDtypeStruct((rows, width), jnp.bfloat16),
-            jax.ShapeDtypeStruct(weight.shape, jnp.float32),
+            pltpu.VMEM((rows, width), jnp.bfloat16),
+            pltpu.VMEM(weight.shape, jnp.float32),
         ),
         in_specs=[pl.BlockSpec(memory_space=pltpu.SMEM)] + [hbm] * 4,
         out_specs=(vmem, vmem),

time: 48.1 us -> 45.5 us (0.946)
  local copies, waits for them, and re-layouts: 3.14 us -> 1.33 us
  Pallas kernels: 44.1 us -> 43.4 us
    unnamed x2, local copies, waits for them, and re-layouts: 3.14 us -> 1.33 us
    pallas_call x1, Pallas kernels: 44.1 us -> 43.4 us  [kernel_shards(): pl.pallas_call(functools.partial(kernel, n_dom, n_rep, inv_scale), out_sh...]
where the time goes in v6:
time: 45.5 us; the launch traced here: 45.3 us
  Pallas kernels  43.4 us (95%)
  local copies, waits for them, and re-layouts  1.33 us (3%)
  between operations  0.64 us (1%)
    pallas_call x1, Pallas kernels, kernel_shards(): pl.pallas_call(functools.partial(kernel, n_dom, n_rep, inv_scale), out_sh...  43.4 us
    unnamed x2, local copies, waits for them, and re-layouts  1.33 us

profile of v6, /device:TPU:1, one launch (start us, length us, event | category | flops | bytes accessed | tf_op | source)
XLA Modules:
  0.0 45.3 jit_solution(8223524977767996843)
XLA Ops:
  0.6 43.4 %shard_map.68 = (bf16[128,256]{1,0:T(8,128)(2,1)S(1)}, f32[256,256]{1,0:T(8,128)S(1)}) custom-call(s32[1,2,16]{2,1,0:T(2,128)} %bitcast.1, bf16[128,256]{1,0:T(8,128)(2,1)} %features_hbm.1, bf16[1,16,2,128,128]{4,3,2,1,0:T(8,128)(2,1)} %values_hbm.1, bf16[256,256]{1,0:T(8,128)(2,1)} %weight_hbm.1, bf16[128,256]{1,0:T(8,128)(2,1)} %cotangent_hbm.1), custom_call_target="tpu_custom_call" | custom-call | tf_op jit(solution)/shard_map/pallas_call | solution.py:288
  44.0 0.6 %copy.9 = bf16[128,256]{1,0:T(8,128)(2,1)} copy(bf16[128,256]{1,0:T(8,128)(2,1)S(1)} %get-tuple-element.2) | data formatting | bytes 131072
  44.6 0.7 %copy.10 = f32[256,256]{1,0:T(8,128)} copy(f32[256,256]{1,0:T(8,128)S(1)} %get-tuple-element.3) | data formatting | bytes 524288

commit v7 on v6

--- a/solution.py
+++ b/solution.py
@@ -12,6 +12,7 @@
 FACE = 4
 SUBLANES = 16
 LANES = 128
+REST = 4
 VMEM_BYTES = 60 * 1024 * 1024
 
 
@@ -59,7 +60,7 @@
     feature_grad_ref, weight_grad_ref,
     values_ref, weight_ref, cotangent_ref, panels, grad_panels, part_out, part_in,
     weight_part, weight_in1, weight_sum1, weight_in2, weight_sum2, weight_in3, weight_out,
-    local_sem, line_send, line_recv, full_send, full_recv, half_send, half_recv,
+    local_sem, face_send, face_recv, slab_send, slab_recv, line_send, line_recv, full_send, full_recv, half_send, half_recv,
     part_send, part_recv, weight_send, weight_recv,
 ):
     rows = cotangent_ref.shape[0]
@@ -99,17 +100,35 @@
     pl.semaphore_wait(barrier, len(partners))
 
     sends = Sends()
-    half = rows // 2
+    most = rows - rows // REST
+    half = most // 2
 
     def gather(which, held):
+        main = pl.ds(0, most)
+        rest = pl.ds(most, rows - most)
         halves = (pl.ds(0, half), pl.ds(half, half))
 
+        def over_face():
+            own = held.at[dom, rest]
+            for j in range(1, FACE):
+                slot = (which, j - 1)
+                sends.start(own, own, face_send.at[slot], face_recv.at[slot], face_to[j])
+
+        def slab_along():
+            for j in range(1, FACE):
+                slot = (which, j - 1)
+                arrived(held.at[face_ids[j], rest], face_send.at[slot], face_recv.at[slot], face_to[j])
+            slab = held.at[pl.ds(z * FACE, FACE), rest]
+            for k in range(1, line):
+                slot = (which, k - 1)
+                sends.start(slab, slab, slab_send.at[slot], slab_recv.at[slot], line_to[k])
+
         def along(k):
-            own = held.at[dom]
+            own = held.at[dom, main]
             sends.start(own, own, line_send.at[which, k - 1], line_recv.at[which, k - 1], line_to[k])
 
         def to_neighbours(k):
-            piece = held.at[line_ids[k]]
+            piece = held.at[line_ids[k], main]
             for way in range(2):
                 slot = (which, way, k)
                 sends.start(piece, piece, full_send.at[slot], full_recv.at[slot], face_to[way + 1])
@@ -118,7 +137,7 @@
             for way in range(2):
                 panel = panel_at(flip(z, k), flip(face, way + 1))
                 slot = (which, way, k)
-                arrived(held.at[panel], full_send.at[slot], full_recv.at[slot], face_to[way + 1])
+                arrived(held.at[panel, main], full_send.at[slot], full_recv.at[slot], face_to[way + 1])
                 piece = held.at[panel, halves[way]]
                 slot = (which, 1 - way, k)
                 sends.start(piece, piece, half_send.at[slot], half_recv.at[slot], face_to[2 - way])
@@ -126,20 +145,23 @@
         def begin():
             for k in range(1, line):
                 along(k)
+            over_face()
             to_neighbours(0)
 
         def own_diagonal():
             to_diagonal(0)
 
         def middle(k):
-            arrived(held.at[line_ids[k]], line_send.at[which, k - 1], line_recv.at[which, k - 1], line_to[k])
+            piece = held.at[line_ids[k], main]
+            arrived(piece, line_send.at[which, k - 1], line_recv.at[which, k - 1], line_to[k])
             to_neighbours(k)
+            if k == line - 1:
+                slab_along()
             if k > 1:
                 to_diagonal(k - 1)
 
         def last():
-            if line > 1:
-                to_diagonal(line - 1)
+            to_diagonal(line - 1)
 
         def finish():
             for k in range(line):
@@ -149,6 +171,10 @@
                     arrived(
                         held.at[panel, halves[1 - way]], half_send.at[slot], half_recv.at[slot], face_to[way + 1]
                     )
+            for k in range(1, line):
+                slot = (which, k - 1)
+                slab = held.at[pl.ds(flip(z, k) * FACE, FACE), rest]
+                arrived(slab, slab_send.at[slot], slab_recv.at[slot], line_to[k])
 
         steps = [begin, own_diagonal]
         steps += [functools.partial(middle, k) for k in range(1, line)]
@@ -309,6 +335,8 @@
             pltpu.VMEM((steps, 2 * face_rows // line, wide // 2), jnp.float32),
             pltpu.VMEM(weight.shape, jnp.bfloat16),
             dma((4,)),
+            dma((2, FACE - 1)), dma((2, FACE - 1)),
+            dma(line_slots), dma(line_slots),
             dma(line_slots), dma(line_slots),
             dma(face_slots), dma(face_slots),
             dma(face_slots), dma(face_slots),
@@ -358,7 +386,7 @@
         and line > 1
         and weight.shape[0] % (2 * SUBLANES * line * n_rep) == 0
         and weight.shape[0] % (2 * LANES) == 0
-        and features.shape[0] % (2 * SUBLANES) == 0
+        and features.shape[0] % (2 * SUBLANES * REST) == 0
     )
     body = kernel_shards if splits else plain_shards
     return body(features, block_values, block_columns, weight, cotangent)

time: 45.5 us -> 46.2 us (1.015)
  Pallas kernels: 43.4 us -> 44.1 us
    pallas_call x1, Pallas kernels: 43.4 us -> 44.1 us  [kernel_shards(): pl.pallas_call(functools.partial(kernel, n_dom, n_rep, inv_scale), out_sh...]
where the time goes in v7:
time: 46.2 us; the launch traced here: 46 us
  Pallas kernels  44.1 us (95%)
  local copies, waits for them, and re-layouts  1.33 us (3%)
  between operations  0.64 us (1%)
    pallas_call x1, Pallas kernels, kernel_shards(): pl.pallas_call(functools.partial(kernel, n_dom, n_rep, inv_scale), out_sh...  44.1 us
    unnamed x2, local copies, waits for them, and re-layouts  1.33 us

profile of v7, /device:TPU:1, one launch (start us, length us, event | category | flops | bytes accessed | tf_op | source)
XLA Modules:
  0.0 46.0 jit_solution(6887250266389300435)
XLA Ops:
  0.6 44.1 %shard_map.68 = (bf16[128,256]{1,0:T(8,128)(2,1)S(1)}, f32[256,256]{1,0:T(8,128)S(1)}) custom-call(s32[1,2,16]{2,1,0:T(2,128)} %bitcast.1, bf16[128,256]{1,0:T(8,128)(2,1)} %features_hbm.1, bf16[1,16,2,128,128]{4,3,2,1,0:T(8,128)(2,1)} %values_hbm.1, bf16[256,256]{1,0:T(8,128)(2,1)} %weight_hbm.1, bf16[128,256]{1,0:T(8,128)(2,1)} %cotangent_hbm.1), custom_call_target="tpu_custom_call" | custom-call | tf_op jit(solution)/shard_map/pallas_call | solution.py:314
  44.7 0.6 %copy.9 = bf16[128,256]{1,0:T(8,128)(2,1)} copy(bf16[128,256]{1,0:T(8,128)(2,1)S(1)} %get-tuple-element.2) | data formatting | bytes 131072
  45.3 0.7 %copy.10 = f32[256,256]{1,0:T(8,128)} copy(f32[256,256]{1,0:T(8,128)S(1)} %get-tuple-element.3) | data formatting | bytes 524288

commit v8 on v6

--- a/solution.py
+++ b/solution.py
@@ -59,7 +59,7 @@
     feature_grad_ref, weight_grad_ref,
     values_ref, weight_ref, cotangent_ref, panels, grad_panels, part_out, part_in,
     weight_part, weight_in1, weight_sum1, weight_in2, weight_sum2, weight_in3, weight_out,
-    local_sem, line_send, line_recv, full_send, full_recv, half_send, half_recv,
+    local_sem, line_send, line_recv, face_send, face_recv,
     part_send, part_recv, weight_send, weight_recv,
 ):
     rows = cotangent_ref.shape[0]
@@ -99,61 +99,35 @@
     pl.semaphore_wait(barrier, len(partners))
 
     sends = Sends()
-    half = rows // 2
 
     def gather(which, held):
-        halves = (pl.ds(0, half), pl.ds(half, half))
-
         def along(k):
             own = held.at[dom]
             sends.start(own, own, line_send.at[which, k - 1], line_recv.at[which, k - 1], line_to[k])
 
-        def to_neighbours(k):
+        def over_face(k):
             piece = held.at[line_ids[k]]
-            for way in range(2):
-                slot = (which, way, k)
-                sends.start(piece, piece, full_send.at[slot], full_recv.at[slot], face_to[way + 1])
-
-        def to_diagonal(k):
-            for way in range(2):
-                panel = panel_at(flip(z, k), flip(face, way + 1))
-                slot = (which, way, k)
-                arrived(held.at[panel], full_send.at[slot], full_recv.at[slot], face_to[way + 1])
-                piece = held.at[panel, halves[way]]
-                slot = (which, 1 - way, k)
-                sends.start(piece, piece, half_send.at[slot], half_recv.at[slot], face_to[2 - way])
+            for j in (3, 1, 2):
+                slot = (which, j - 1, k)
+                sends.start(piece, piece, face_send.at[slot], face_recv.at[slot], face_to[j])
 
         def begin():
             for k in range(1, line):
                 along(k)
-            to_neighbours(0)
-
-        def own_diagonal():
-            to_diagonal(0)
+            over_face(0)
 
         def middle(k):
             arrived(held.at[line_ids[k]], line_send.at[which, k - 1], line_recv.at[which, k - 1], line_to[k])
-            to_neighbours(k)
-            if k > 1:
-                to_diagonal(k - 1)
-
-        def last():
-            if line > 1:
-                to_diagonal(line - 1)
+            over_face(k)
 
         def finish():
             for k in range(line):
-                panel = panel_at(flip(z, k), flip(face, 3))
-                for way in range(2):
-                    slot = (which, way, k)
-                    arrived(
-                        held.at[panel, halves[1 - way]], half_send.at[slot], half_recv.at[slot], face_to[way + 1]
-                    )
-
-        steps = [begin, own_diagonal]
-        steps += [functools.partial(middle, k) for k in range(1, line)]
-        steps += [last, finish]
-        return steps
+                for j in range(1, FACE):
+                    slot = (which, j - 1, k)
+                    panel = held.at[panel_at(flip(z, k), flip(face, j))]
+                    arrived(panel, face_send.at[slot], face_recv.at[slot], face_to[j])
+
+        return [begin] + [functools.partial(middle, k) for k in range(1, line)] + [finish]
 
     def block_product(held, a):
         left = jnp.concatenate([values_ref[t, a] for t in range(rounds)], axis=1)
@@ -244,19 +218,16 @@
         hidden, grad_pre, (((0,), (0,)), ((), ())), preferred_element_type=jnp.float32
     )
     sems1 = exchange(weight_part, weight_in1, rep_to, [span(i * rep_rows, rep_rows) for i in rep_ids])
-    back[1]()
     weight_sum1[...] = take(weight_in1, sems1, rep_to, weight_part[span(rep_base, rep_rows)])
     sems2 = exchange(weight_sum1, weight_in2, face_to, [span(f * face_rows, face_rows) for f in face_f])
-    for step in back[2:3]:
-        step()
+    back[1]()
     weight_sum2[...] = take(weight_in2, sems2, face_to, weight_sum1[span(face * face_rows, face_rows)])
     sems3 = exchange(weight_sum2, weight_in3, line_to, [tile(0, i) for i in line_z])
-    for step in back[3:-2]:
+    for step in back[2:-1]:
         step()
     own_sum = take(weight_in3, sems3, line_to, weight_sum2[tile(0, z)])
     weight_out[tile(face_base, z)] = (own_sum * inv_scale).astype(jnp.bfloat16)
     sems4 = share(tile(face_base, z), line_to)
-    back[-2]()
     collect([tile(face_base, i) for i in line_z], sems4, line_to)
     sems5 = share(span(face_base, face_rows), face_to)
     back[-1]()
@@ -283,7 +254,7 @@
     vmem = pl.BlockSpec(memory_space=pltpu.VMEM)
     hbm = pl.BlockSpec(memory_space=pl.ANY)
     dma = pltpu.SemaphoreType.DMA
-    face_slots = (2, 2, line)
+    face_slots = (2, FACE - 1, line)
     line_slots = (2, steps)
     return pl.pallas_call(
         functools.partial(kernel, n_dom, n_rep, inv_scale),
@@ -311,7 +282,6 @@
             dma((4,)),
             dma(line_slots), dma(line_slots),
             dma(face_slots), dma(face_slots),
-            dma(face_slots), dma(face_slots),
             dma((2, parts)), dma((2, parts)),
             dma((weight_copies,)), dma((weight_copies,)),
         ],
@@ -358,7 +328,7 @@
         and line > 1
         and weight.shape[0] % (2 * SUBLANES * line * n_rep) == 0
         and weight.shape[0] % (2 * LANES) == 0
-        and features.shape[0] % (2 * SUBLANES) == 0
+        and features.shape[0] % SUBLANES == 0
     )
     body = kernel_shards if splits else plain_shards
     return body(features, block_values, block_columns, weight, cotangent)

time: 45.5 us -> 42.4 us (0.932)
  Pallas kernels: 43.4 us -> 40.3 us
    pallas_call x1, Pallas kernels: 43.4 us -> 40.3 us  [kernel_shards(): pl.pallas_call(functools.partial(kernel, n_dom, n_rep, inv_scale), out_sh...]
where the time goes in v8:
time: 42.4 us; the launch traced here: 42.3 us
  Pallas kernels  40.3 us (95%)
  local copies, waits for them, and re-layouts  1.33 us (3%)
  between operations  0.64 us (2%)
    pallas_call x1, Pallas kernels, kernel_shards(): pl.pallas_call(functools.partial(kernel, n_dom, n_rep, inv_scale), out_sh...  40.3 us
    unnamed x2, local copies, waits for them, and re-layouts  1.33 us

profile of v8, /device:TPU:1, one launch (start us, length us, event | category | flops | bytes accessed | tf_op | source)
XLA Modules:
  0.0 42.3 jit_solution(15143691190643403278)
XLA Ops:
  0.6 40.3 %shard_map.68 = (bf16[128,256]{1,0:T(8,128)(2,1)S(1)}, f32[256,256]{1,0:T(8,128)S(1)}) custom-call(s32[1,2,16]{2,1,0:T(2,128)} %bitcast.1, bf16[128,256]{1,0:T(8,128)(2,1)} %features_hbm.1, bf16[1,16,2,128,128]{4,3,2,1,0:T(8,128)(2,1)} %values_hbm.1, bf16[256,256]{1,0:T(8,128)(2,1)} %weight_hbm.1, bf16[128,256]{1,0:T(8,128)(2,1)} %cotangent_hbm.1), custom_call_target="tpu_custom_call" | custom-call | tf_op jit(solution)/shard_map/pallas_call | solution.py:259
  40.9 0.6 %copy.9 = bf16[128,256]{1,0:T(8,128)(2,1)} copy(bf16[128,256]{1,0:T(8,128)(2,1)S(1)} %get-tuple-element.2) | data formatting | bytes 131072
  41.6 0.7 %copy.10 = f32[256,256]{1,0:T(8,128)} copy(f32[256,256]{1,0:T(8,128)S(1)} %get-tuple-element.3) | data formatting | bytes 524288

commit v9 on v8

--- a/solution.py
+++ b/solution.py
@@ -112,7 +112,7 @@
                 sends.start(piece, piece, face_send.at[slot], face_recv.at[slot], face_to[j])
 
         def begin():
-            for k in range(1, line):
+            for k in range(line - 1, 0, -1):
                 along(k)
             over_face(0)
 

time: 42.4 us -> 43.4 us (1.024)
  Pallas kernels: 40.3 us -> 41.3 us
    pallas_call x1, Pallas kernels: 40.3 us -> 41.3 us  [kernel_shards(): pl.pallas_call(functools.partial(kernel, n_dom, n_rep, inv_scale), out_sh...]
where the time goes in v9:
time: 43.4 us; the launch traced here: 43.2 us
  Pallas kernels  41.3 us (95%)
  local copies, waits for them, and re-layouts  1.33 us (3%)
  between operations  0.64 us (1%)
    pallas_call x1, Pallas kernels, kernel_shards(): pl.pallas_call(functools.partial(kernel, n_dom, n_rep, inv_scale), out_sh...  41.3 us
    unnamed x2, local copies, waits for them, and re-layouts  1.33 us

profile of v9, /device:TPU:1, one launch (start us, length us, event | category | flops | bytes accessed | tf_op | source)
XLA Modules:
  0.0 43.2 jit_solution(5227375159494662978)
XLA Ops:
  0.6 41.3 %shard_map.68 = (bf16[128,256]{1,0:T(8,128)(2,1)S(1)}, f32[256,256]{1,0:T(8,128)S(1)}) custom-call(s32[1,2,16]{2,1,0:T(2,128)} %bitcast.1, bf16[128,256]{1,0:T(8,128)(2,1)} %features_hbm.1, bf16[1,16,2,128,128]{4,3,2,1,0:T(8,128)(2,1)} %values_hbm.1, bf16[256,256]{1,0:T(8,128)(2,1)} %weight_hbm.1, bf16[128,256]{1,0:T(8,128)(2,1)} %cotangent_hbm.1), custom_call_target="tpu_custom_call" | custom-call | tf_op jit(solution)/shard_map/pallas_call | solution.py:259
  41.9 0.6 %copy.9 = bf16[128,256]{1,0:T(8,128)(2,1)} copy(bf16[128,256]{1,0:T(8,128)(2,1)S(1)} %get-tuple-element.2) | data formatting | bytes 131072
  42.5 0.7 %copy.10 = f32[256,256]{1,0:T(8,128)} copy(f32[256,256]{1,0:T(8,128)S(1)} %get-tuple-element.3) | data formatting | bytes 524288

commit v10 on v8

--- a/solution.py
+++ b/solution.py
@@ -107,7 +107,7 @@
 
         def over_face(k):
             piece = held.at[line_ids[k]]
-            for j in (3, 1, 2):
+            for j in (1, 2, 3):
                 slot = (which, j - 1, k)
                 sends.start(piece, piece, face_send.at[slot], face_recv.at[slot], face_to[j])
 

time: 42.4 us -> 43 us (1.014)
  Pallas kernels: 40.3 us -> 40.9 us
    pallas_call x1, Pallas kernels: 40.3 us -> 40.9 us  [kernel_shards(): pl.pallas_call(functools.partial(kernel, n_dom, n_rep, inv_scale), out_sh...]
where the time goes in v10:
time: 43 us; the launch traced here: 42.9 us
  Pallas kernels  40.9 us (95%)
  local copies, waits for them, and re-layouts  1.33 us (3%)
  between operations  0.64 us (1%)
    pallas_call x1, Pallas kernels, kernel_shards(): pl.pallas_call(functools.partial(kernel, n_dom, n_rep, inv_scale), out_sh...  40.9 us
    unnamed x2, local copies, waits for them, and re-layouts  1.33 us

profile of v10, /device:TPU:1, one launch (start us, length us, event | category | flops | bytes accessed | tf_op | source)
XLA Modules:
  0.0 42.9 jit_solution(16961464143986848418)
XLA Ops:
  0.6 40.9 %shard_map.68 = (bf16[128,256]{1,0:T(8,128)(2,1)S(1)}, f32[256,256]{1,0:T(8,128)S(1)}) custom-call(s32[1,2,16]{2,1,0:T(2,128)} %bitcast.1, bf16[128,256]{1,0:T(8,128)(2,1)} %features_hbm.1, bf16[1,16,2,128,128]{4,3,2,1,0:T(8,128)(2,1)} %values_hbm.1, bf16[256,256]{1,0:T(8,128)(2,1)} %weight_hbm.1, bf16[128,256]{1,0:T(8,128)(2,1)} %cotangent_hbm.1), custom_call_target="tpu_custom_call" | custom-call | tf_op jit(solution)/shard_map/pallas_call | solution.py:259
  41.5 0.6 %copy.9 = bf16[128,256]{1,0:T(8,128)(2,1)} copy(bf16[128,256]{1,0:T(8,128)(2,1)S(1)} %get-tuple-element.2) | data formatting | bytes 131072
  42.2 0.7 %copy.10 = f32[256,256]{1,0:T(8,128)} copy(f32[256,256]{1,0:T(8,128)S(1)} %get-tuple-element.3) | data formatting | bytes 524288
